TPU v7x, 128 devices: a whole 4x4x4 slice. The times are simulated.
128 devices in a mesh: dp: 8 (over z, core), seq: 16 (over x, y).
Axes of the slice: x: 4, y: 4, z: 4, core: 2. Of those that a mesh axis runs over, the one named last changes fastest.
Arguments:
- q_proj: bfloat16 [16384, 8192], P(('dp', 'seq')), may hold values from -6 to 6
- k_proj: bfloat16 [16384, 1024], P(('dp', 'seq')), may hold values from -6 to 6
- v_proj: bfloat16 [16384, 1024], P(('dp', 'seq')), may hold values from -6 to 6
- q_gain: float32 [128], replicated, may hold values from 0.5 to 6
- k_gain: float32 [128], replicated, may hold values from 0.5 to 6
- dout: bfloat16 [16384, 8192], P(('dp', 'seq')), may hold values from -7 to 7
- segments: int32 [16384], replicated, may hold values from 0 to 7, as said below
Outputs:
- attn_out: bfloat16 [16384, 8192], P(('dp', 'seq'))
- q_grad: bfloat16 [16384, 8192], P(('dp', 'seq'))
- k_grad: bfloat16 [16384, 1024], P(('dp', 'seq'))
- v_grad: bfloat16 [16384, 1024], P(('dp', 'seq'))
- q_gain_grad: float32 [128], replicated
- k_gain_grad: float32 [128], replicated
Inputs may be any that keep to these rules, and one draw needn't show every extreme that they name: `segments`: along each packed row of 2048 tokens the ids never fall and start at 0; of the two rows 2i and 2i + 1 one holds a single rollout filling the row and the other exactly 8 rollouts.
All inputs are finite; a program needn't handle non-finite values.
Results may differ from a plain program's by a relative error of at most 0.017.
The roundings to bfloat16 on the way count: a program that leaves them out, or rounds other values in their place, can miss the bound.
Values may be sent and summed in bfloat16 or wider, within the bound.
A program may use at most 192 MiB of HBM per device.

v0:
```python
import math

import jax
import jax.numpy as jnp
from jax import lax
from jax.sharding import PartitionSpec as P

QH = 64
KVH = 8
HD = 128


tile_span = 512
neg_fill = -1e30
norm_eps = 1e-06


def tile_scores(q_part, keys, key_ids, ids_part, positions, kblock, k_tile, scale):
    k_part = lax.dynamic_slice_in_dim(keys, kblock * k_tile, k_tile, 0)
    ids_key = lax.dynamic_slice_in_dim(key_ids, kblock * k_tile, k_tile, 0)
    key_pos = kblock * k_tile + jnp.arange(k_tile, dtype=jnp.int32)
    allowed = (ids_part[:, None] == ids_key[None, :]) & (key_pos[None, :] <= positions[:, None])
    allowed = allowed[:, None, None, :]
    scores = (
        jnp.einsum("qgrd,kgd->qgrk", q_part, k_part, preferred_element_type=jnp.float32) * scale
    )
    return (jnp.where(allowed, scores, neg_fill), allowed)


def tile_live(key_ids, ids_part, positions, kblock, k_tile):
    first_key = kblock * k_tile
    last_id = lax.dynamic_index_in_dim(key_ids, first_key + k_tile - 1, 0, keepdims=False)
    return (first_key <= positions[-1]) & (last_id >= ids_part[0])


def attend(queries, keys, values, upstream, query_ids, key_ids, query_start):
    q_len, groups, ratio, head_dim = queries.shape
    k_len = keys.shape[0]
    q_tile = min(tile_span, q_len)
    k_tile = min(tile_span, k_len)
    k_count = k_len // k_tile
    scale = 1.0 / math.sqrt(head_dim)
    key_grad = jnp.zeros((k_len, groups, head_dim), jnp.float32)
    value_grad = jnp.zeros((k_len, groups, head_dim), jnp.float32)
    outputs = []
    query_grads = []
    for block in range(q_len // q_tile):
        q_part = queries[block * q_tile : (block + 1) * q_tile]
        g_part = upstream[block * q_tile : (block + 1) * q_tile]
        ids_part = query_ids[block * q_tile : (block + 1) * q_tile]
        positions = query_start + block * q_tile + jnp.arange(q_tile, dtype=jnp.int32)

        def stat_step(kblock, carry):

            def stat_update(state):
                top, total = state
                masked, allowed = tile_scores(
                    q_part, keys, key_ids, ids_part, positions, kblock, k_tile, scale
                )
                new_top = jnp.maximum(top, jnp.max(masked, axis=-1))
                weights = jnp.where(allowed, jnp.exp(masked - new_top[..., None]), 0.0)
                return (new_top, total * jnp.exp(top - new_top) + jnp.sum(weights, axis=-1))

            return lax.cond(
                tile_live(key_ids, ids_part, positions, kblock, k_tile),
                stat_update,
                lambda state: state,
                carry,
            )

        start_top = jnp.full((q_tile, groups, ratio), neg_fill, jnp.float32)
        start_total = jnp.zeros((q_tile, groups, ratio), jnp.float32)
        top, total = lax.fori_loop(
            jnp.int32(0), jnp.int32(k_count), stat_step, (start_top, start_total)
        )
        logsum = top + jnp.log(total)

        def out_step(kblock, carry):

            def out_update(accum):
                masked, allowed = tile_scores(
                    q_part, keys, key_ids, ids_part, positions, kblock, k_tile, scale
                )
                v_part = lax.dynamic_slice_in_dim(values, kblock * k_tile, k_tile, 0)
                probs = jnp.exp(masked - logsum[..., None]).astype(jnp.bfloat16)
                return accum + jnp.einsum(
                    "qgrk,kgd->qgrd", probs, v_part, preferred_element_type=jnp.float32
                )

            return lax.cond(
                tile_live(key_ids, ids_part, positions, kblock, k_tile),
                out_update,
                lambda accum: accum,
                carry,
            )

        accum = lax.fori_loop(
            jnp.int32(0),
            jnp.int32(k_count),
            out_step,
            jnp.zeros((q_tile, groups, ratio, head_dim), jnp.float32),
        )
        out_part = accum.astype(jnp.bfloat16)
        delta = jnp.sum(g_part.astype(jnp.float32) * out_part.astype(jnp.float32), axis=-1)

        def grad_step(kblock, carry):

            def grad_update(state):
                q_acc, k_acc, v_acc = state
                masked, allowed = tile_scores(
                    q_part, keys, key_ids, ids_part, positions, kblock, k_tile, scale
                )
                k_part = lax.dynamic_slice_in_dim(keys, kblock * k_tile, k_tile, 0)
                v_part = lax.dynamic_slice_in_dim(values, kblock * k_tile, k_tile, 0)
                exact = jnp.exp(masked - logsum[..., None])
                probs = exact.astype(jnp.bfloat16)
                dprob = jnp.einsum(
                    "qgrd,kgd->qgrk", g_part, v_part, preferred_element_type=jnp.float32
                )
                dscore = (exact * (dprob - delta[..., None]) * scale).astype(jnp.bfloat16)
                q_acc = q_acc + jnp.einsum(
                    "qgrk,kgd->qgrd", dscore, k_part, preferred_element_type=jnp.float32
                )
                k_tile_grad = jnp.einsum(
                    "qgrk,qgrd->kgd", dscore, q_part, preferred_element_type=jnp.float32
                )
                v_tile_grad = jnp.einsum(
                    "qgrk,qgrd->kgd", probs, g_part, preferred_element_type=jnp.float32
                )
                first_key = kblock * k_tile
                k_acc = lax.dynamic_update_slice_in_dim(
                    k_acc,
                    lax.dynamic_slice_in_dim(k_acc, first_key, k_tile, 0) + k_tile_grad,
                    first_key,
                    0,
                )
                v_acc = lax.dynamic_update_slice_in_dim(
                    v_acc,
                    lax.dynamic_slice_in_dim(v_acc, first_key, k_tile, 0) + v_tile_grad,
                    first_key,
                    0,
                )
                return (q_acc, k_acc, v_acc)

            return lax.cond(
                tile_live(key_ids, ids_part, positions, kblock, k_tile),
                grad_update,
                lambda state: state,
                carry,
            )

        start_q = jnp.zeros((q_tile, groups, ratio, head_dim), jnp.float32)
        q_acc, key_grad, value_grad = lax.fori_loop(
            jnp.int32(0), jnp.int32(k_count), grad_step, (start_q, key_grad, value_grad)
        )
        outputs.append(out_part)
        query_grads.append(q_acc)
    return (
        jnp.concatenate(outputs, axis=0),
        jnp.concatenate(query_grads, axis=0),
        key_grad,
        value_grad,
    )


def normalize(raw, gain):
    inverse = lax.rsqrt(jnp.mean(raw * raw, axis=-1, keepdims=True) + norm_eps)
    hatted = raw * inverse
    return (hatted, inverse, (hatted * gain).astype(jnp.bfloat16))


def norm_backward(grad_norm, hatted, inverse, gain):
    scaled = grad_norm * gain
    return (inverse * (scaled - hatted * jnp.mean(scaled * hatted, axis=-1, keepdims=True))).astype(
        jnp.bfloat16
    )


def on_device(q_proj, k_proj, v_proj, q_gain, k_gain, dout, segments):
    local_rows = q_proj.shape[0]
    seq_count = lax.axis_size("seq")
    seq_len = local_rows * seq_count
    total_rows = seq_len * lax.axis_size("dp")
    raw_q = q_proj.reshape(local_rows, QH, HD)
    raw_k = k_proj.reshape(local_rows, KVH, HD)
    k_hat, k_inv, k_norm = normalize(raw_k.astype(jnp.float32), k_gain)
    values = v_proj.reshape(local_rows, KVH, HD)
    upstream = dout.reshape(local_rows, QH, HD)
    row_index = lax.axis_index("dp")
    row_ids = lax.dynamic_slice_in_dim(segments, row_index * seq_len, seq_len, 0)
    q_grad = None
    q_gain_local = None
    repeats = seq_count // KVH
    value_slots = jnp.repeat(values, repeats, axis=1)
    q_hat, q_inv, q_norm = normalize(raw_q.astype(jnp.float32), q_gain)
    send_k = jnp.repeat(k_norm, repeats, axis=1)
    head_q, head_g, head_k, head_v = (
        lax.all_to_all(q_norm, "seq", split_axis=1, concat_axis=0, tiled=True),
        lax.all_to_all(upstream, "seq", split_axis=1, concat_axis=0, tiled=True),
        lax.all_to_all(send_k, "seq", split_axis=1, concat_axis=0, tiled=True),
        lax.all_to_all(value_slots, "seq", split_axis=1, concat_axis=0, tiled=True),
    )
    per_dev = head_q.shape[1]
    head_q = head_q.reshape(seq_len, 1, per_dev, HD)
    head_g = head_g.reshape(seq_len, 1, per_dev, HD)
    head_out, head_qg, head_kg, head_vg = attend(
        head_q, head_k, head_v, head_g, row_ids, row_ids, 0
    )
    head_qg = head_qg.reshape(seq_len, per_dev, HD)
    attn_local = lax.all_to_all(
        head_out.reshape(seq_len, per_dev, HD), "seq", split_axis=0, concat_axis=1, tiled=True
    )
    q_norm_grad, key_back, value_back = (
        lax.all_to_all(
            head_qg.astype(jnp.bfloat16), "seq", split_axis=0, concat_axis=1, tiled=True
        ).astype(head_qg.dtype),
        lax.all_to_all(
            head_kg.astype(jnp.bfloat16), "seq", split_axis=0, concat_axis=1, tiled=True
        ).astype(head_kg.dtype),
        lax.all_to_all(
            head_vg.astype(jnp.bfloat16), "seq", split_axis=0, concat_axis=1, tiled=True
        ).astype(head_vg.dtype),
    )
    k_norm_grad = jnp.sum(key_back.reshape(local_rows, KVH, repeats, HD), axis=2)
    v_sum = jnp.sum(value_back.reshape(local_rows, KVH, repeats, HD), axis=2)
    q_grad = norm_backward(q_norm_grad, q_hat, q_inv, q_gain)
    q_gain_local = jnp.sum(q_norm_grad * q_hat, axis=(0, 1))
    k_grad = norm_backward(k_norm_grad, k_hat, k_inv, k_gain)
    k_gain_local = jnp.sum(k_norm_grad * k_hat, axis=(0, 1))
    q_gain_sum, k_gain_sum = lax.psum((q_gain_local, k_gain_local), ("dp", "seq"))
    q_gain_grad = q_gain_sum / math.sqrt(total_rows * QH)
    k_gain_grad = k_gain_sum / math.sqrt(total_rows * KVH)
    return (
        attn_local.reshape(local_rows, QH * HD),
        q_grad.reshape(local_rows, QH * HD),
        k_grad.reshape(local_rows, KVH * HD),
        v_sum.astype(jnp.bfloat16).reshape(local_rows, KVH * HD),
        q_gain_grad,
        k_gain_grad,
    )


def solution(mesh):
    return jax.shard_map(
        on_device,
        mesh=mesh,
        in_specs=(
            P(("dp", "seq"), None),
            P(("dp", "seq"), None),
            P(("dp", "seq"), None),
            P(),
            P(),
            P(("dp", "seq"), None),
            P(),
        ),
        out_specs=(
            P(("dp", "seq"), None),
            P(("dp", "seq"), None),
            P(("dp", "seq"), None),
            P(("dp", "seq"), None),
            P(),
            P(),
        ),
        check_vma=False,
    )
```

profile of v0, /device:TPU:0, one launch (start us, length us, event | category | flops | bytes accessed | tf_op | source)
XLA Modules:
  0.0 664.3 jit_solution(8902475596842231145)
XLA Ops:
  3.9 7.1 %all-to-all-start.1 = ((bf16[128,16,128]{2,0,1:T(8,128)(2,1)}), bf16[128,16,128]{2,0,1:T(8,128)(2,1)S(1)}, u32[]{:S(2)}, u32[]{:S(2)}) async-start(bf16[128,16,128]{2,0,1:T(8,128)(2,1)} %bitcast.181), calls=%async_computation.1 | async-start | bytes 1048576 | tf_op jit(solution)/shard_map/all_to_all | solution.py:200
  17.0 5.5 all-to-all-done.1
  41.0 4.1 copy.294
  45.0 23.8 %all-to-all-done.2 = bf16[128,64,128]{2,0,1:T(8,128)(2,1)S(1)} async-done(((bf16[128,64,128]{2,0,1:T(8,128)(2,1)}), bf16[128,64,128]{2,0,1:T(8,128)(2,1)S(1)}, u32[]{:S(2)}, u32[]{:S(2)}) %all-to-all-start.2) | async-done | bytes 2097184 | tf_op jit(solution)/shard_map/all_to_all | solution.py:198
  70.1 4.4 all-to-all-start.4
  80.4 17.4 %while.216 = (s32[]{:T(128)}, f32[512,1,4]{0,2,1:T(4,128)S(1)}, f32[512,1,4]{0,2,1:T(4,128)S(1)}, s32[512]{0:T(512)S(1)}, s32[2048]{0:T(1024)S(1)}, /*index=5*/s...) while((s32[]{:T(128)}, f32[512,1,4]{0,2,1:T(4,128)S(1)}, ...), condition=%wide.region_7.8_spmd.clone, body=%wide.region_2.7_spmd.clone.sunk | while | flops 277615104 | bytes 9951631 | solution.py:73
  99.0 19.7 %while.217 = (s32[]{:T(128)}, f32[512,1,4,128]{0,3,2,1:T(8,128)}, s32[512]{0:T(512)S(1)}, s32[2048]{0:T(1024)S(1)}, s32[512]{0:T(512)S(1)}, /*index=5*/bf16[2048...) while((s32[]{:T(128)}, f32[512,1,4,128]{0,3,2,1:T(8,128)}, ...), condition=%wide.region_11.12_spmd.clone, body=%wide.region_8.11_spmd.clone.sunk | while | flops 542114304 | bytes 3431803 | solution.py:97
  102.8 4.3 conditional.37
  103.2 3.9 fusion.14
  128.6 23.0 %while.224 = (s32[]{:T(128)}, f32[512,1,4,128]{0,3,2,1:T(8,128)S(1)}, f32[2048,1,128]{2,0,1:T(8,128)S(1)}, f32[2048,1,128]{2,0,1:T(8,128)}, s32[512]{0:T(512)S(1...) while((s32[]{:T(128)}, ...), condition=%wide.region_46.47_spmd.clone, body=%wide.region_43.46_spmd.clone.sunk | while | flops 1354891776 | bytes 27433500 | solution.py:153
  132.4 7.8 %conditional.44 = ((f32[512,1,4,128]{0,3,2,1:T(8,128)S(1)}, f32[2048,1,128]{2,0,1:T(8,128)S(1)}, f32[2048,1,128]{2,0,1:T(8,128)})) conditional(s32[]{:T(128)} %convert_element_type.504, (f32[512,1,4,128]{0,3,2,1:T(8,128)S(1)}, f32[2048,1,128]{2,0,1:T(8,128)S(1)}, f32[2048,1,128]{2,0,1:T(8,128)}) %tuple.595, (s32[]{:T(128)}, ...), branch_computations={%region_44.44_spmd, %region_45.45_spmd} | conditional | flops 1354891776 | bytes 27433094 | solution.py:145
  153.1 20.0 %while.218 = (s32[]{:T(128)}, f32[512,1,4]{0,2,1:T(4,128)S(1)}, f32[512,1,4]{0,2,1:T(4,128)S(1)}, s32[512]{0:T(512)S(1)}, s32[2048]{0:T(1024)S(1)}, /*index=5*/s...) while((s32[]{:T(128)}, f32[512,1,4]{0,2,1:T(4,128)S(1)}, ...), condition=%wide.region_17.18_spmd.clone, body=%wide.region_12.17_spmd.clone.sunk | while | flops 277615104 | bytes 9951631 | solution.py:73
  174.2 23.5 %while.219 = (s32[]{:T(128)}, f32[512,1,4,128]{0,3,2,1:T(8,128)}, s32[512]{0:T(512)S(1)}, s32[2048]{0:T(1024)S(1)}, s32[512]{0:T(512)S(1)}, /*index=5*/bf16[2048...) while((s32[]{:T(128)}, f32[512,1,4,128]{0,3,2,1:T(8,128)}, ...), condition=%wide.region_21.0_spmd.clone, body=%wide.region_18.21_spmd.clone.sunk | while | flops 542114304 | bytes 3431803 | solution.py:97
  178.0 4.3 conditional.39
  178.3 3.9 fusion.43
  186.0 4.3 conditional.39
  186.4 3.9 fusion.43
  201.5 29.6 %while.225 = (s32[]{:T(128)}, f32[512,1,4,128]{0,3,2,1:T(8,128)S(1)}, f32[2048,1,128]{2,0,1:T(8,128)S(1)}, f32[2048,1,128]{2,0,1:T(8,128)}, s32[512]{0:T(512)S(1...) while((s32[]{:T(128)}, ...), condition=%wide.region_51.0_spmd.clone, body=%wide.region_48.51_spmd.clone.sunk | while | flops 1354891776 | bytes 27433500 | solution.py:153
  205.0 7.8 %conditional.45 = ((f32[512,1,4,128]{0,3,2,1:T(8,128)S(1)}, f32[2048,1,128]{2,0,1:T(8,128)S(1)}, f32[2048,1,128]{2,0,1:T(8,128)})) conditional(s32[]{:T(128)} %convert_element_type.505, (f32[512,1,4,128]{0,3,2,1:T(8,128)S(1)}, f32[2048,1,128]{2,0,1:T(8,128)S(1)}, f32[2048,1,128]{2,0,1:T(8,128)}) %tuple.598, (s32[]{:T(128)}, ...), branch_computations={%region_49.49_spmd, %region_50.50_spmd} | conditional | flops 1354891776 | bytes 27433094 | solution.py:145
  216.3 7.8 %conditional.45 = ((f32[512,1,4,128]{0,3,2,1:T(8,128)S(1)}, f32[2048,1,128]{2,0,1:T(8,128)S(1)}, f32[2048,1,128]{2,0,1:T(8,128)})) conditional(s32[]{:T(128)} %convert_element_type.505, (f32[512,1,4,128]{0,3,2,1:T(8,128)S(1)}, f32[2048,1,128]{2,0,1:T(8,128)S(1)}, f32[2048,1,128]{2,0,1:T(8,128)}) %tuple.598, (s32[]{:T(128)}, ...), branch_computations={%region_49.49_spmd, %region_50.50_spmd} | conditional | flops 1354891776 | bytes 27433094 | solution.py:145
  232.6 20.1 %while.220 = (s32[]{:T(128)}, f32[512,1,4]{0,2,1:T(4,128)S(1)}, f32[512,1,4]{0,2,1:T(4,128)S(1)}, s32[512]{0:T(512)S(1)}, s32[2048]{0:T(1024)S(1)}, /*index=5*/s...) while((s32[]{:T(128)}, f32[512,1,4]{0,2,1:T(4,128)S(1)}, ...), condition=%wide.region_27.28_spmd.clone, body=%wide.region_22.27_spmd.clone.sunk | while | flops 277615104 | bytes 9951631 | solution.py:73
  252.8 20.8 %while.221 = (s32[]{:T(128)}, f32[512,1,4,128]{0,3,2,1:T(8,128)S(1)}, s32[512]{0:T(512)S(1)}, s32[2048]{0:T(1024)S(1)}, s32[512]{0:T(512)S(1)}, /*index=5*/bf16[...) while((s32[]{:T(128)}, ...), condition=%wide.region_31.32_spmd.clone, body=%wide.region_28.31_spmd.clone.sunk | while | flops 542114304 | bytes 3431803 | solution.py:97
  278.3 34.4 %while.226 = (s32[]{:T(128)}, f32[512,1,4,128]{0,3,2,1:T(8,128)S(1)}, f32[2048,1,128]{2,0,1:T(8,128)}, f32[2048,1,128]{2,0,1:T(8,128)}, s32[512]{0:T(512)S(1)}, ...) while((s32[]{:T(128)}, ...), condition=%wide.region_56.57_spmd.clone, body=%wide.region_53.56_spmd.clone.sunk | while | flops 1354891776 | bytes 27433500 | solution.py:153
  286.1 9.5 %conditional.46 = ((f32[512,1,4,128]{0,3,2,1:T(8,128)S(1)}, f32[2048,1,128]{2,0,1:T(8,128)}, f32[2048,1,128]{2,0,1:T(8,128)})) conditional(s32[]{:T(128)} %convert_element_type.506, (f32[512,1,4,128]{0,3,2,1:T(8,128)S(1)}, f32[2048,1,128]{2,0,1:T(8,128)}, f32[2048,1,128]{2,0,1:T(8,128)}) %tuple.601, (s32[]{:T(128)}, ...), branch_computations={%region_54.54_spmd, %region_55.55_spmd} | conditional | flops 1354891776 | bytes 27433094 | solution.py:145
  299.4 9.5 %conditional.46 = ((f32[512,1,4,128]{0,3,2,1:T(8,128)S(1)}, f32[2048,1,128]{2,0,1:T(8,128)}, f32[2048,1,128]{2,0,1:T(8,128)})) conditional(s32[]{:T(128)} %convert_element_type.506, (f32[512,1,4,128]{0,3,2,1:T(8,128)S(1)}, f32[2048,1,128]{2,0,1:T(8,128)}, f32[2048,1,128]{2,0,1:T(8,128)}) %tuple.601, (s32[]{:T(128)}, ...), branch_computations={%region_54.54_spmd, %region_55.55_spmd} | conditional | flops 1354891776 | bytes 27433094 | solution.py:145
  313.9 21.7 %while.222 = (s32[]{:T(128)}, f32[512,1,4]{0,2,1:T(4,128)S(1)}, f32[512,1,4]{0,2,1:T(4,128)S(1)}, s32[512]{0:T(512)S(1)}, s32[2048]{0:T(1024)S(1)}, /*index=5*/s...) while((s32[]{:T(128)}, f32[512,1,4]{0,2,1:T(4,128)S(1)}, ...), condition=%wide.region_37.38_spmd.clone, body=%wide.region_32.37_spmd.clone.sunk | while | flops 277615104 | bytes 9951631 | solution.py:73
  336.7 27.6 %while.223 = (s32[]{:T(128)}, f32[512,1,4,128]{0,3,2,1:T(8,128)}, s32[512]{0:T(512)S(1)}, s32[2048]{0:T(1024)S(1)}, s32[512]{0:T(512)S(1)}, /*index=5*/bf16[2048...) while((s32[]{:T(128)}, f32[512,1,4,128]{0,3,2,1:T(8,128)}, ...), condition=%wide.region_41.42_spmd.clone, body=%wide.region_38.41_spmd.clone.sunk | while | flops 542114304 | bytes 3431803 | solution.py:97
  344.1 4.3 conditional.43
  344.4 3.9 fusion.101
  352.0 4.3 conditional.43
  359.9 4.3 conditional.43
  360.3 3.9 fusion.101
  370.4 43.9 %while.227 = (s32[]{:T(128)}, f32[512,1,4,128]{0,3,2,1:T(8,128)}, f32[2048,1,128]{2,0,1:T(8,128)}, f32[2048,1,128]{2,0,1:T(8,128)}, s32[512]{0:T(512)S(1)}, /*in...) while((s32[]{:T(128)}, f32[512,1,4,128]{0,3,2,1:T(8,128)}, ...), condition=%wide.region_61.62_spmd.clone, body=%wide.region_58.61_spmd.clone.sunk | while | flops 1354891776 | bytes 35822164 | solution.py:153
  377.7 9.8 %conditional.47 = ((f32[512,1,4,128]{0,3,2,1:T(8,128)}, f32[2048,1,128]{2,0,1:T(8,128)}, f32[2048,1,128]{2,0,1:T(8,128)})) conditional(s32[]{:T(128)} %convert_element_type.507, (f32[512,1,4,128]{0,3,2,1:T(8,128)}, f32[2048,1,128]{2,0,1:T(8,128)}, f32[2048,1,128]{2,0,1:T(8,128)}) %tuple.604, (s32[]{:T(128)}, bf16[2048,1,128]{2,0,1:T(8,128)(2,1)S(1)}, ...), branch_computations={%region_59.59_spmd, %region_60.60_spmd} | conditional | flops 1354891776 | bytes 35821760 | solution.py:145
  391.1 9.8 %conditional.47 = ((f32[512,1,4,128]{0,3,2,1:T(8,128)}, f32[2048,1,128]{2,0,1:T(8,128)}, f32[2048,1,128]{2,0,1:T(8,128)})) conditional(s32[]{:T(128)} %convert_element_type.507, (f32[512,1,4,128]{0,3,2,1:T(8,128)}, f32[2048,1,128]{2,0,1:T(8,128)}, f32[2048,1,128]{2,0,1:T(8,128)}) %tuple.604, (s32[]{:T(128)}, bf16[2048,1,128]{2,0,1:T(8,128)(2,1)S(1)}, ...), branch_computations={%region_59.59_spmd, %region_60.60_spmd} | conditional | flops 1354891776 | bytes 35821760 | solution.py:145
  404.5 9.8 %conditional.47 = ((f32[512,1,4,128]{0,3,2,1:T(8,128)}, f32[2048,1,128]{2,0,1:T(8,128)}, f32[2048,1,128]{2,0,1:T(8,128)})) conditional(s32[]{:T(128)} %convert_element_type.507, (f32[512,1,4,128]{0,3,2,1:T(8,128)}, f32[2048,1,128]{2,0,1:T(8,128)}, f32[2048,1,128]{2,0,1:T(8,128)}) %tuple.604, (s32[]{:T(128)}, bf16[2048,1,128]{2,0,1:T(8,128)(2,1)S(1)}, ...), branch_computations={%region_59.59_spmd, %region_60.60_spmd} | conditional | flops 1354891776 | bytes 35821760 | solution.py:145
  421.7 7.3 %all-to-all-start.6 = ((bf16[16,2,8192]{2,1,0:T(2,128)(2,1)}), bf16[16,2,8192]{2,1,0:T(2,128)(2,1)}, u32[]{:S(2)}, u32[]{:S(2)}) async-start(bf16[16,2,8192]{2,1,0:T(2,128)(2,1)} %reshape.1151), calls=%async_computation.6 | async-start | bytes 1048576 | tf_op jit(solution)/shard_map/all_to_all | solution.py:217
  434.6 4.5 all-to-all-done.6
  439.2 4.5 all-to-all-start.7
  448.1 13.2 %maximum_bitcast_fusion.1 = bf16[2048,4,128]{2,1,0:T(4,128)(2,1)} fusion(bf16[512,1,4,128]{3,2,0,1:T(4,128)(2,1)} %copy.303, bf16[512,1,4,128]{3,2,0,1:T(4,128)(2,1)} %copy.301, bf16[512,1,4,128]{3,2,0,1:T(4,128)(2,1)S(1)} %copy.299, bf16[512,1,4,128]{3,2,0,1:T(4,128)(2,1)S(1)} %copy.297), kind=kLoop, calls=%fused_computation.298 | loop fusion | flops 3145728 | bytes 4194304 | tf_op jit(solution)/shard_map/convert_element_type | solution.py:215
  461.2 7.7 %all-to-all-start.5 = ((bf16[2048,4,128]{2,1,0:T(4,128)(2,1)}), bf16[2048,4,128]{2,1,0:T(4,128)(2,1)S(1)}, u32[]{:S(2)}, u32[]{:S(2)}) async-start(bf16[2048,4,128]{2,1,0:T(4,128)(2,1)} %maximum_bitcast_fusion.1), calls=%async_computation.5 | async-start | bytes 4194304 | tf_op jit(solution)/shard_map/all_to_all | solution.py:214
  470.4 5.6 copy.307
  477.4 10.7 %copy.292 = bf16[2048,4,128]{2,1,0:T(4,128)(2,1)} copy(bf16[2048,4,128]{2,0,1:T(8,128)(2,1)S(1)} %maximum_bitcast_fusion) | data formatting | bytes 4194304 | tf_op jit(solution)/shard_map/reshape | solution.py:211
  504.9 7.5 %all-to-all-start.3 = ((bf16[2048,4,128]{2,1,0:T(4,128)(2,1)}), bf16[2048,4,128]{2,1,0:T(4,128)(2,1)}, u32[]{:S(2)}, u32[]{:S(2)}) async-start(bf16[2048,4,128]{2,1,0:T(4,128)(2,1)} %copy.292), calls=%async_computation.3 | async-start | bytes 4194304 | tf_op jit(solution)/shard_map/all_to_all | solution.py:210
  516.3 28.2 %fusion.331 = (f32[128]{0:T(128)S(1)}, f32[128,16,4]{2,1,0:T(8,128)S(1)}) fusion(f32[16,128,4,128]{3,2,1,0:T(4,128)S(1)} %get-tuple-element.3846, f32[128,16,4,128]{3,2,1,0:T(4,128)S(1)} %copy-done.9, f32[128,16,4]{2,1,0:T(8,128)S(1)} %copy-done.22, f32[128]{0:T(128)S(1)} %copy-done.39), kind=kLoop, calls=%fused_computation.292 | loop fusion | flops 6283136 | bytes 8455168 | tf_op jit(solution)/shard_map/reduce_sum | solution.py:227
  545.0 5.5 copy.305
  554.3 4.1 copy.315
  558.4 99.1 %all-reduce = (f32[128]{0:T(128)S(1)}, f32[128]{0:T(128)S(1)}) all-reduce(f32[128]{0:T(128)S(1)} %get-tuple-element.3592, f32[128]{0:T(128)S(1)} %bitcast_reduce_fusion), channel_id=1, replica_groups=mesh['dp'=8,'seq'=16] {'dp','seq'}, use_global_device_ids=true, to_apply=%region_67.68 | all-reduce | flops 256 | bytes 2048 | tf_op jit(solution)/shard_map/psum | solution.py:230
  (536 shorter events, 329.2 us)
Async XLA Ops:
  0.6 13.6 %copy-start = (bf16[128,1024]{1,0:T(8,128)(2,1)S(1)}, bf16[128,1024]{1,0:T(8,128)(2,1)}, u32[]{:S(2)}) copy-start(bf16[128,1024]{1,0:T(8,128)(2,1)} %param.57) | copy-start | bytes 786436
  1.8 2.1 copy-start.20
  1.9 2.0 copy-start.36
  2.1 1.8 copy-start.11
  3.9 18.6 %all-to-all-start.1 = ((bf16[128,16,128]{2,0,1:T(8,128)(2,1)}), bf16[128,16,128]{2,0,1:T(8,128)(2,1)S(1)}, u32[]{:S(2)}, u32[]{:S(2)}) async-start(bf16[128,16,128]{2,0,1:T(8,128)(2,1)} %bitcast.181), calls=%async_computation.1 | async-start | bytes 1048576 | tf_op jit(solution)/shard_map/all_to_all | solution.py:200
  14.2 9.1 %copy-start.7 = (bf16[128,8192]{0,1:T(8,128)(2,1)}, bf16[128,8192]{0,1:T(8,128)(2,1)S(1)}, u32[]{:S(2)}) copy-start(bf16[128,8192]{0,1:T(8,128)(2,1)S(1)} %copy.276) | copy-start | bytes 6291460
  14.3 13.3 %copy-start.38 = (f32[128]{0:T(128)S(1)}, f32[128]{0:T(128)}, u32[]{:S(2)}) copy-start(f32[128]{0:T(128)} %param.58) | copy-start | bytes 1540
  23.4 13.8 %all-to-all-start = ((bf16[128,16,128]{2,0,1:T(8,128)(2,1)}), bf16[128,16,128]{2,0,1:T(8,128)(2,1)S(1)}, u32[]{:S(2)}, u32[]{:S(2)}) async-start(bf16[128,16,128]{2,0,1:T(8,128)(2,1)} %bitcast.932), calls=%async_computation | async-start | bytes 1048576 | tf_op jit(solution)/shard_map/all_to_all | solution.py:201
  37.2 39.4 %copy-start.23 = (bf16[128,16,128]{2,0,1:T(8,128)(2,1)}, bf16[128,16,128]{2,0,1:T(8,128)(2,1)S(1)}, u32[]{:S(2)}) copy-start(bf16[128,16,128]{2,0,1:T(8,128)(2,1)S(1)} %all-to-all-done) | copy-start | bytes 1572868
  37.2 31.6 %all-to-all-start.2 = ((bf16[128,64,128]{2,0,1:T(8,128)(2,1)}), bf16[128,64,128]{2,0,1:T(8,128)(2,1)S(1)}, u32[]{:S(2)}, u32[]{:S(2)}) async-start(bf16[128,64,128]{2,0,1:T(8,128)(2,1)} %copy.279), calls=%async_computation.2 | async-start | bytes 4194304 | tf_op jit(solution)/shard_map/all_to_all | solution.py:198
  68.8 1.3 copy-start.10
  70.1 50.7 %all-to-all-start.4 = ((bf16[128,64,128]{0,2,1:T(8,128)(2,1)}), bf16[128,64,128]{0,2,1:T(8,128)(2,1)S(1)}, u32[]{:S(2)}, u32[]{:S(2)}) async-start(bf16[128,64,128]{0,2,1:T(8,128)(2,1)} %bitcast.201), calls=%async_computation.4 | async-start | bytes 4194304 | tf_op jit(solution)/shard_map/all_to_all | solution.py:199
  123.7 2.8 copy-start.13
  151.6 1.5 copy-start.2
  199.3 1.7 copy-start.15
  205.0 1.1 copy-start.29
  216.3 1.1 copy-start.29
  231.1 1.5 copy-start.6
  276.1 1.7 copy-start.17
  278.3 35.5 %copy-start.32 = (s32[512]{0:T(512)S(1)}, s32[512]{0:T(512)}, u32[]{:S(2)}) copy-start(s32[512]{0:T(512)} %get-tuple-element.5167) | copy-start | bytes 6148
  278.3 35.5 %copy-start.33 = (s32[512]{0:T(512)S(1)}, s32[512]{0:T(512)}, u32[]{:S(2)}) copy-start(s32[512]{0:T(512)} %get-tuple-element.5165) | copy-start | bytes 6148
  286.1 1.1 copy-start.31
  299.4 1.1 copy-start.31
  367.7 2.7 copy-start.24
  378.8 5.1 copy-start.4
  384.4 3.1 copy-start.5
  392.2 5.1 copy-start.4
  397.8 3.1 copy-start.5
  405.6 5.1 copy-start.4
  411.2 3.1 copy-start.5
  414.3 14.7 %copy-start.18 = (f32[2048,1,128]{2,0,1:T(8,128)S(1)}, f32[2048,1,128]{2,0,1:T(8,128)}, u32[]{:S(2)}) copy-start(f32[2048,1,128]{2,0,1:T(8,128)} %get-tuple-element.3013) | copy-start | bytes 3145732
  421.7 17.5 %all-to-all-start.6 = ((bf16[16,2,8192]{2,1,0:T(2,128)(2,1)}), bf16[16,2,8192]{2,1,0:T(2,128)(2,1)}, u32[]{:S(2)}, u32[]{:S(2)}) async-start(bf16[16,2,8192]{2,1,0:T(2,128)(2,1)} %reshape.1151), calls=%async_computation.6 | async-start | bytes 1048576 | tf_op jit(solution)/shard_map/all_to_all | solution.py:217
  429.9 17.8 %copy-start.3 = (f32[512,1,4,128]{0,3,2,1:T(8,128)S(1)}, f32[512,1,4,128]{0,3,2,1:T(8,128)}, u32[]{:S(2)}) copy-start(f32[512,1,4,128]{0,3,2,1:T(8,128)} %copy-done.2) | copy-start | bytes 3145732
  439.2 22.1 %all-to-all-start.7 = ((bf16[16,2,8192]{2,1,0:T(2,128)(2,1)}), bf16[16,2,8192]{2,1,0:T(2,128)(2,1)}, u32[]{:S(2)}, u32[]{:S(2)}) async-start(bf16[16,2,8192]{2,1,0:T(2,128)(2,1)} %reshape.1153), calls=%async_computation.7 | async-start | bytes 1048576 | tf_op jit(solution)/shard_map/all_to_all | solution.py:220
  448.1 20.9 %copy-start.35 = (f32[128,64]{0,1:T(8,128)S(1)}, f32[128,64]{0,1:T(8,128)}, u32[]{:S(2)}) copy-start(f32[128,64]{0,1:T(8,128)} %copy-done.34) | copy-start | bytes 98308
  461.2 43.6 %all-to-all-start.5 = ((bf16[2048,4,128]{2,1,0:T(4,128)(2,1)}), bf16[2048,4,128]{2,1,0:T(4,128)(2,1)S(1)}, u32[]{:S(2)}, u32[]{:S(2)}) async-start(bf16[2048,4,128]{2,1,0:T(4,128)(2,1)} %maximum_bitcast_fusion.1), calls=%async_computation.5 | async-start | bytes 4194304 | tf_op jit(solution)/shard_map/all_to_all | solution.py:214
  470.4 5.6 copy-start.40
  470.4 5.6 copy-start.39
  470.4 5.6 copy-start.14
  470.4 5.7 copy-start.16
  488.1 8.8 %copy-start.12 = (f32[128,8,128]{2,0,1:T(8,128)S(1)}, f32[128,8,128]{2,0,1:T(8,128)}, u32[]{:S(2)}) copy-start(f32[128,8,128]{2,0,1:T(8,128)} %copy-done.11) | copy-start | bytes 1572868
  488.1 8.8 %copy-start.37 = (f32[128,8]{0,1:T(8,128)S(1)}, f32[128,8]{0,1:T(8,128)}, u32[]{:S(2)}) copy-start(f32[128,8]{0,1:T(8,128)} %copy-done.36) | copy-start | bytes 12292
  488.1 9.2 %copy-start.21 = (bf16[128,1024]{0,1:T(8,128)(2,1)S(1)}, bf16[128,1024]{0,1:T(8,128)(2,1)}, u32[]{:S(2)}) copy-start(bf16[128,1024]{0,1:T(8,128)(2,1)} %copy-done.20) | copy-start | bytes 786436
  504.9 153.6 %all-to-all-start.3 = ((bf16[2048,4,128]{2,1,0:T(4,128)(2,1)}), bf16[2048,4,128]{2,1,0:T(4,128)(2,1)}, u32[]{:S(2)}, u32[]{:S(2)}) async-start(bf16[2048,4,128]{2,1,0:T(4,128)(2,1)} %copy.292), calls=%async_computation.3 | async-start | bytes 4194304 | tf_op jit(solution)/shard_map/all_to_all | solution.py:210
  512.4 3.1 copy-start.9
  512.5 3.9 copy-start.22
  545.0 5.5 copy-start.8
  658.5 5.6 copy-start.1
  (9 other events, 8.3 us)
where the time goes:
time: 673 us; the launch traced here: 664 us
  local copies, waits for them, and re-layouts  188 us (28%)
  matrix products  104 us (15%)
  blocking collectives  99.1 us (15%)
  loops' own time  96.2 us (14%)
  other arithmetic  92.3 us (14%)
  starting transfers between devices  45.9 us (7%)
  waiting for transfers between devices  37.6 us (6%)
    psum x1, blocking collectives, on_device(): lax.psum((q_gain_local, k_gain_local), ('dp', 'seq'))  99.1 us
    slice x96, local copies, waits for them, and re-layouts, tile_live(): return (first_key <= positions[-1]) & (last_id >= ids_part[0])  55.7 us
    another operation x4, loops' own time, attend(): lax.fori_loop(jnp.int32(0), jnp.int32(k_count), stat_step, (start_top, st...  32.6 us
    another operation x4, loops' own time, attend(): lax.fori_loop(jnp.int32(0), jnp.int32(k_count), out_step, jnp.zeros((q_ti...  31.4 us
    unnamed x82, local copies, waits for them, and re-layouts  30.9 us
    another operation x4, loops' own time, attend(): lax.fori_loop(jnp.int32(0), jnp.int32(k_count), grad_step, (start_q, key_...  30.7 us
    dynamic_slice x48, local copies, waits for them, and re-layouts, tile_live(): lax.dynamic_index_in_dim(key_ids, first_key + k_tile - 1, 0, keepdims=False)  29 us
    dot_general x8, matrix products, out_update(): jnp.einsum('qgrk,kgd->qgrd', probs, v_part, preferred_element_type=jnp.fl...  28.5 us
  transfers between devices with their start and end apart: 8, of which 4 were waited for; matrix products, arithmetic and copies ran while one was open for 23% of the time, Pallas kernels for 0%

commit v1 on v0

v1 whole, which is shorter than its diff:
```python
import math

import jax
import jax.numpy as jnp
from jax import lax
from jax.experimental import pallas as pl
from jax.experimental.pallas import tpu as pltpu
from jax.sharding import PartitionSpec as P

QH = 64
KVH = 8
HD = 128
EPS = 1e-06
NEG = -1e30
MESH = pl.DeviceIdType.MESH
BLK = 128
SIDE = 4
PART = 4096
OWN = 1024
CH = 512
KT = 256
SCALE = 1.0 / math.sqrt(HD)
LOG2E = math.log2(math.e)
bf16 = jnp.bfloat16
f32 = jnp.float32


def dot_nt(a, b):
    return lax.dot_general(a, b, (((1,), (1,)), ((), ())), preferred_element_type=f32)


def dot_nn(a, b):
    return lax.dot_general(a, b, (((1,), (0,)), ((), ())), preferred_element_type=f32)


def fold(x, op):
    rows, cols = x.shape
    return op(x.reshape(rows // 8, 8, cols), axis=0)


def kernel(
    q, k, v, do, seg, qg, kg,
    o, dq, dk, dv, qgp, kgp,
    qs, ds_, kv, kn, vn, kt_, vt_, os_, dqs, es, ms, firsts, dka, dva, sb, rb, fb, qn, ot, dqt, gacc,
    s_in, r_in, s_kv, r_kv, s_ag, r_ag, s_out, r_out, s_rs, r_rs, s_f, r_f,
):
    seq = lax.axis_index("seq")
    dp = lax.axis_index("dp")
    x, y = seq // SIDE, seq % SIDE
    mine = (x, y)

    def where(p, j):
        return (dp, lax.select(p == 0, j * SIDE + y, x * SIDE + j))

    def own(p):
        return lax.select(p == 0, x, y)

    def remote(src, dst, ss, rs, dev):
        return pltpu.make_async_remote_copy(
            src_ref=src, dst_ref=dst, send_sem=ss, recv_sem=rs, device_id=dev, device_id_type=MESH
        )

    def cols(start, width):
        return pl.ds(pl.multiple_of(start, width), width)

    barrier = pltpu.get_barrier_semaphore()
    for p in (0, 1):
        for d in (1, 2, 3):
            j = (mine[p] + d) % SIDE
            dev = (dp, j * SIDE + y) if p == 0 else (dp, x * SIDE + j)
            pl.semaphore_signal(barrier, inc=1, device_id=dev, device_id_type=MESH)

    for p in (0, 1):
        me = mine[p]
        for i, src in enumerate((k, v)):
            pltpu.make_async_copy(
                src.at[:, cols(p * 512 + me * HD, HD)], kv.at[p, i, x, y], r_kv.at[p, i, me]
            ).start()
    pl.semaphore_wait(barrier, 6)

    def dev_of(p, j):
        return (dp, j * SIDE + y) if p == 0 else (dp, x * SIDE + j)

    kv_sends = []
    for d in (1, 3, 2):
        for p in (0, 1):
            me = mine[p]
            j = (me + d) % SIDE
            for i, src in enumerate((k, v)):
                c = remote(
                    src.at[:, cols(p * 512 + j * HD, HD)], kv.at[p, i, x, y],
                    s_kv.at[p, i, d], r_kv.at[p, i, me], dev_of(p, j),
                )
                c.start()
                kv_sends.append(c)

    for p in (0, 1):
        me = mine[p]
        for i, src in enumerate((q, do)):
            dst = (qs, ds_)[i]
            for c in (0, 1):
                pltpu.make_async_copy(
                    src.at[:, cols(p * PART + me * OWN + c * CH, CH)],
                    dst.at[p, me, c], r_in.at[i, p, me, c],
                ).start()

    ag_sends = []
    for p in (0, 1):
        me = mine[p]
        other = mine[1 - p]
        for j in range(SIDE):
            for i in (0, 1):
                blk = kv.at[p, i, j, y] if p == 0 else kv.at[p, i, x, j]
                pltpu.make_async_copy(blk, blk, r_kv.at[p, i, j]).wait()
        held = kv.at[0, :, :, y] if p == 0 else kv.at[1, :, x]
        for d in (1, 3, 2):
            c = remote(
                held, held, s_ag.at[p, d], r_ag.at[p, other], dev_of(1 - p, (other + d) % SIDE)
            )
            c.start()
            ag_sends.append(c)

    in_sends = []
    for c in (0, 1):
        for d in (1, 3, 2):
            for p in (0, 1):
                me = mine[p]
                j = (me + d) % SIDE
                for i, src in enumerate((q, do)):
                    dst = (qs, ds_)[i]
                    cp = remote(
                        src.at[:, cols(p * PART + j * OWN + c * CH, CH)], dst.at[p, me, c],
                        s_in.at[i, p, d, c], r_in.at[i, p, me, c], dev_of(p, j),
                    )
                    cp.start()
                    in_sends.append(cp)

    ids = seg[...]
    first = jnp.zeros((16, BLK), jnp.int32)
    for value in range(7):
        hits = jnp.where(ids == value, 1, 0)
        count = jnp.sum(jnp.sum(hits, axis=1, keepdims=True), axis=0, keepdims=True)
        first = first + jnp.where(ids > value, count, 0)
    seg_first = first

    dka[...] = jnp.zeros_like(dka)
    dva[...] = jnp.zeros_like(dva)
    gacc[...] = jnp.zeros_like(gacc)
    for i in range(16):
        firsts[i] = seg_first[i : i + 1, :]

    for p in (0, 1):
        other = mine[1 - p]
        for d in (1, 3, 2):
            j = (other + d) % SIDE
            blk = kv.at[0, :, :, j] if p == 0 else kv.at[1, :, j]
            pltpu.make_async_copy(blk, blk, r_ag.at[p, j]).wait()

    def prep(t, carry):
        p, b = t // 16, t % 16
        raw = kv[p, 0, b // SIDE, b % SIDE].astype(f32)
        inv = lax.rsqrt(jnp.mean(raw * raw, axis=-1, keepdims=True) + EPS)
        normed = (raw * inv * kg[...]).astype(bf16)
        rows = cols(b * BLK, BLK)
        kn[p, rows, :] = normed
        kt_[p, :, rows] = normed.astype(f32).T.astype(bf16)
        val = kv[p, 1, b // SIDE, b % SIDE]
        vn[p, rows, :] = val
        vt_[p, :, rows] = val.astype(f32).T.astype(bf16)
        return carry

    lax.fori_loop(0, 32, prep, 0)

    def unit(u, carry):
        c = u // 8
        p = u % 2
        step = (u % 8) // 2
        d = lax.select(step == 2, 3, lax.select(step == 3, 2, step))
        me = own(p)
        j = (me + d) % SIDE
        b = lax.select(p == 0, j * SIDE + y, x * SIDE + j)
        n_tiles = b // 2 + 1
        for i, dst in enumerate((qs, ds_)):
            blk = dst.at[p, j, c]
            pltpu.make_async_copy(blk, blk, r_in.at[i, p, j, c]).wait()

        for h in range(4):
            raw = qs[p, j, c, :, h * HD : (h + 1) * HD].astype(f32)
            inv = lax.rsqrt(jnp.mean(raw * raw, axis=-1, keepdims=True) + EPS)
            qn[0, h * BLK : (h + 1) * BLK, :] = (raw * inv * qg[...]).astype(bf16)
            qn[1, h * BLK : (h + 1) * BLK, :] = ds_[p, j, c, :, h * HD : (h + 1) * HD]

        q_pos = b * BLK + lax.broadcasted_iota(jnp.int32, (1, BLK), 1)
        q_first = firsts[b]

        def scores(t, carry):
            top, total = carry
            rows = cols(t * KT, KT)
            s = dot_nt(kn[p, rows, :], qn[0])
            k_pos = t * KT + lax.broadcasted_iota(jnp.int32, (KT, BLK), 0)
            allowed = (k_pos >= q_first) & (k_pos <= q_pos)
            s = jnp.concatenate(
                [jnp.where(allowed, s[:, h * BLK : (h + 1) * BLK], NEG) for h in range(4)], axis=1
            )
            new = jnp.maximum(top, jnp.max(fold(s, jnp.max), axis=0, keepdims=True))
            e = jnp.exp2((s - new) * (SCALE * LOG2E))
            es[rows, :] = e
            ms[t] = new
            total = total * jnp.exp2((top - new) * (SCALE * LOG2E)) + fold(e, jnp.sum)
            return new, total

        top, total = lax.fori_loop(
            0, n_tiles, scores, (jnp.full((1, CH), NEG, f32), jnp.zeros((8, CH), f32))
        )
        recip = 1.0 / jnp.sum(total, axis=0, keepdims=True)

        ot[...] = jnp.zeros_like(ot)

        def outs(t, carry):
            rows = cols(t * KT, KT)
            factor = jnp.exp2((ms[t] - top) * (SCALE * LOG2E)) * recip
            e = es[rows, :] * factor
            es[rows, :] = e
            pr = e.astype(bf16)
            ot[...] += dot_nn(vt_[p, :, rows], pr)
            dva[p, rows, :] += dot_nn(pr, qn[1])
            return carry

        lax.fori_loop(0, n_tiles, outs, 0)

        deltas = []
        for h in range(4):
            out = ot[:, h * BLK : (h + 1) * BLK].T.astype(bf16)
            os_[p, j, c, :, h * HD : (h + 1) * HD] = out
            up = qn[1, h * BLK : (h + 1) * BLK, :].astype(f32)
            deltas.append(jnp.sum((up * out.astype(f32)).T, axis=0, keepdims=True))
        delta = jnp.concatenate(deltas, axis=1)

        dqt[...] = jnp.zeros_like(dqt)

        def grads(t, carry):
            rows = cols(t * KT, KT)
            dp_ = dot_nt(vn[p, rows, :], qn[1])
            g = (es[rows, :] * (dp_ - delta) * SCALE).astype(bf16)
            dqt[...] += dot_nn(kt_[p, :, rows], g)
            dka[p, rows, :] += dot_nn(g, qn[0])
            return carry

        lax.fori_loop(0, n_tiles, grads, 0)

        for h in range(4):
            raw = qs[p, j, c, :, h * HD : (h + 1) * HD].astype(f32)
            inv = lax.rsqrt(jnp.mean(raw * raw, axis=-1, keepdims=True) + EPS)
            hat = raw * inv
            grad = dqt[:, h * BLK : (h + 1) * BLK].T
            gacc[0] += fold(grad * hat, jnp.sum)
            g = grad * qg[...]
            dqs[p, j, c, :, h * HD : (h + 1) * HD] = (
                inv * (g - hat * jnp.mean(g * hat, axis=-1, keepdims=True))
            ).astype(bf16)

        for i, (src, dst) in enumerate(((os_, o), (dqs, dq))):
            place = dst.at[:, cols(p * PART + me * OWN + c * CH, CH)]

            @pl.when(d == 0)
            def _():
                pltpu.make_async_copy(src.at[p, j, c], place, r_out.at[i, p, j, c]).start()

            @pl.when(d != 0)
            def _():
                remote(
                    src.at[p, j, c], place, s_out.at[i, p, d, c], r_out.at[i, p, me, c],
                    where(p, j),
                ).start()

        return carry

    lax.fori_loop(0, 16, unit, 0)

    def pack(t, carry):
        p, b = t // 16, t % 16
        rows = cols(b * BLK, BLK)
        sb[p, 0, b // SIDE, b % SIDE] = dka[p, rows, :].astype(bf16)
        sb[p, 1, b // SIDE, b % SIDE] = dva[p, rows, :].astype(bf16)
        return carry

    rs_sends = []
    for p in (0, 1):
        lax.fori_loop(p * 16, p * 16 + 16, pack, 0)
        other = mine[1 - p]
        for d in (1, 3, 2):
            j = (other + d) % SIDE
            src = sb.at[0, :, :, j] if p == 0 else sb.at[1, :, j]
            c = remote(
                src, rb.at[p, other], s_rs.at[p, d], r_rs.at[p, other], dev_of(1 - p, j)
            )
            c.start()
            rs_sends.append(c)

    f_sends = []
    for p in (0, 1):
        other = mine[1 - p]
        me = mine[p]
        for d in (1, 3, 2):
            blk = rb.at[p, (other + d) % SIDE]
            pltpu.make_async_copy(blk, blk, r_rs.at[p, (other + d) % SIDE]).wait()
        for dd in (1, 3, 2, 0):
            j = (me + dd) % SIDE
            b = j * SIDE + y if p == 0 else x * SIDE + j
            rows = cols(b * BLK, BLK)
            kgrad = dka[p, rows, :]
            vgrad = dva[p, rows, :]
            for d in (1, 2, 3):
                slot = (other + d) % SIDE
                kgrad = kgrad + rb[p, slot, 0, j].astype(f32)
                vgrad = vgrad + rb[p, slot, 1, j].astype(f32)
            raw = (kv[0, 0, j, y] if p == 0 else kv[1, 0, x, j]).astype(f32)
            inv = lax.rsqrt(jnp.mean(raw * raw, axis=-1, keepdims=True) + EPS)
            hat = raw * inv
            gacc[1] += fold(kgrad * hat, jnp.sum)
            g = kgrad * kg[...]
            fb[p, 0, j] = (inv * (g - hat * jnp.mean(g * hat, axis=-1, keepdims=True))).astype(
                bf16
            )
            fb[p, 1, j] = vgrad.astype(bf16)
            for i, dst in enumerate((dk, dv)):
                place = dst.at[:, cols(p * 512 + me * HD, HD)]
                if dd == 0:
                    pltpu.make_async_copy(fb.at[p, i, j], place, r_f.at[p, i, me]).start()
                else:
                    c = remote(
                        fb.at[p, i, j], place, s_f.at[p, i, dd], r_f.at[p, i, me], dev_of(p, j)
                    )
                    c.start()
                    f_sends.append(c)

    qgp[...] = jnp.sum(gacc[0], axis=0, keepdims=True)
    kgp[...] = jnp.sum(gacc[1], axis=0, keepdims=True)

    for c in kv_sends + ag_sends + in_sends + rs_sends + f_sends:
        c.wait_send()

    def drain(t, carry):
        i, p, d, c = t // 12, (t // 6) % 2, (t // 2) % 3 + 1, t % 2
        src = os_.at[0, 0, 0]
        pltpu.make_async_copy(src, src, s_out.at[i, p, d, c]).wait()
        return carry

    lax.fori_loop(0, 24, drain, 0)

    def arrive(t, carry):
        i, p, j, c = t // 16, (t // 8) % 2, (t // 2) % 4, t % 2
        place = o.at[:, cols(p * PART + j * OWN + c * CH, CH)]
        pltpu.make_async_copy(place, place, r_out.at[i, p, j, c]).wait()
        return carry

    lax.fori_loop(0, 32, arrive, 0)
    for p in (0, 1):
        for i, dst in enumerate((dk, dv)):
            for j in range(SIDE):
                place = dst.at[:, cols(p * 512 + j * HD, HD)]
                pltpu.make_async_copy(place, place, r_f.at[p, i, j]).wait()


def on_device(q_proj, k_proj, v_proj, q_gain, k_gain, dout, segments):
    rows = q_proj.shape[0]
    total_rows = rows * lax.axis_size("seq") * lax.axis_size("dp")
    ids = lax.dynamic_index_in_dim(
        segments.reshape(lax.axis_size("dp"), 16, BLK), lax.axis_index("dp"), 0, keepdims=False
    )
    any_ = pl.BlockSpec(memory_space=pl.ANY)
    vmem = pl.BlockSpec(memory_space=pltpu.VMEM)
    dma = pltpu.SemaphoreType.DMA
    length = SIDE * SIDE * BLK
    o, dq, dk, dv, qgp, kgp = pl.pallas_call(
        kernel,
        out_shape=(
            jax.ShapeDtypeStruct((rows, QH * HD), bf16),
            jax.ShapeDtypeStruct((rows, QH * HD), bf16),
            jax.ShapeDtypeStruct((rows, KVH * HD), bf16),
            jax.ShapeDtypeStruct((rows, KVH * HD), bf16),
            jax.ShapeDtypeStruct((1, HD), f32),
            jax.ShapeDtypeStruct((1, HD), f32),
        ),
        in_specs=[any_, any_, any_, any_, vmem, vmem, vmem],
        out_specs=(any_, any_, any_, any_, vmem, vmem),
        scratch_shapes=[
            pltpu.VMEM((2, SIDE, 2, BLK, CH), bf16),
            pltpu.VMEM((2, SIDE, 2, BLK, CH), bf16),
            pltpu.VMEM((2, 2, SIDE, SIDE, BLK, HD), bf16),
            pltpu.VMEM((2, length, HD), bf16),
            pltpu.VMEM((2, length, HD), bf16),
            pltpu.VMEM((2, HD, length), bf16),
            pltpu.VMEM((2, HD, length), bf16),
            pltpu.VMEM((2, SIDE, 2, BLK, CH), bf16),
            pltpu.VMEM((2, SIDE, 2, BLK, CH), bf16),
            pltpu.VMEM((length, CH), f32),
            pltpu.VMEM((8, 1, CH), f32),
            pltpu.VMEM((16, 1, BLK), jnp.int32),
            pltpu.VMEM((2, length, HD), f32),
            pltpu.VMEM((2, length, HD), f32),
            pltpu.VMEM((2, 2, SIDE, SIDE, BLK, HD), bf16),
            pltpu.VMEM((2, SIDE, 2, SIDE, BLK, HD), bf16),
            pltpu.VMEM((2, 2, SIDE, BLK, HD), bf16),
            pltpu.VMEM((2, CH, HD), bf16),
            pltpu.VMEM((HD, CH), f32),
            pltpu.VMEM((HD, CH), f32),
            pltpu.VMEM((2, 8, HD), f32),
            dma((2, 2, SIDE, 2)), dma((2, 2, SIDE, 2)),
            dma((2, 2, SIDE)), dma((2, 2, SIDE)),
            dma((2, SIDE)), dma((2, SIDE)),
            dma((2, 2, SIDE, 2)), dma((2, 2, SIDE, 2)),
            dma((2, SIDE)), dma((2, SIDE)),
            dma((2, 2, SIDE)), dma((2, 2, SIDE)),
        ],
        name="exchange_attend",
        cost_estimate=pl.CostEstimate(
            flops=20_000_000_000, bytes_accessed=20_000_000, transcendentals=10_000_000
        ),
        compiler_params=pltpu.CompilerParams(
            collective_id=0, has_side_effects=True, vmem_limit_bytes=48 << 20
        ),
    )(q_proj, k_proj, v_proj, dout, ids, q_gain.reshape(1, HD), k_gain.reshape(1, HD))
    sums = lax.psum(jnp.concatenate([qgp, kgp], axis=0), ("dp", "seq"))
    return (
        o,
        dq,
        dk,
        dv,
        sums[0] / math.sqrt(total_rows * QH),
        sums[1] / math.sqrt(total_rows * KVH),
    )


def solution(mesh):
    split = P(("dp", "seq"), None)
    return jax.shard_map(
        on_device,
        mesh=mesh,
        in_specs=(split, split, split, P(), P(), split, P()),
        out_specs=(split, split, split, split, P(), P()),
        check_vma=False,
    )
```

time: 673 us -> 259 us (0.38); the launches traced: 664 us -> 258 us
  Pallas kernels: 0 us -> 180 us
  local copies, waits for them, and re-layouts: 188 us -> 11.2 us
  matrix products: 104 us -> 0 us
  loops' own time: 96.2 us -> 0 us
  other arithmetic: 92.3 us -> 0.53 us
  starting transfers between devices: 45.9 us -> 0 us
  waiting for transfers between devices: 37.6 us -> 0 us
  blocking collectives: 99.1 us -> 65.6 us
    pallas_call x0 -> x1, Pallas kernels: none -> 180 us  [on_device(): pl.pallas_call(kernel, out_shape=(jax.ShapeDtypeStruct((rows, QH * HD), b...]
    dot_general x56 -> x0, matrix products: 104 us -> none  [the longest x8 28.5 us: out_update(): jnp.einsum('qgrk,kgd->qgrd', probs, v_part, preferred_element_type=jnp.fl...]
    another operation x60 -> x0, loops' own time: 96.2 us -> none  [the longest x4 32.6 us: attend(): lax.fori_loop(jnp.int32(0), jnp.int32(k_count), stat_step, (start_top, st...]
    slice x106 -> x0, local copies, waits for them, and re-layouts: 68.9 us -> none  [the longest x96 55.7 us: tile_live(): return (first_key <= positions[-1]) & (last_id >= ids_part[0])]
    reduce_sum x20 -> x0, other arithmetic: 46.1 us -> none  [the longest x1 28.2 us: on_device(): q_gain_local = jnp.sum(q_norm_grad * q_hat, axis=(0, 1))]
    all_to_all x8 -> x0, starting transfers between devices: 45.9 us -> none  [the longest x1 7.72 us: on_device(): lax.all_to_all(head_qg.astype(jnp.bfloat16), 'seq', split_axis=0, concat_...]
    all_to_all x8 -> x0, waiting for transfers between devices: 37.6 us -> none  [the longest x1 23.8 us: on_device(): lax.all_to_all(q_norm, 'seq', split_axis=1, concat_axis=0, tiled=True)]
    convert_element_type x10 -> x0, other arithmetic: 35.4 us -> none  [the longest x1 13.2 us: on_device(): head_qg.astype(jnp.bfloat16)]
  transfers between devices with their start and end apart: 8 -> 0, of which waited for: 4 -> 0; matrix products, arithmetic and copies ran while one was open for 23% -> 0% of each run, Pallas kernels for 0% -> 0%
where the time goes in v1:
time: 259 us; the launch traced here: 258 us
  Pallas kernels  180 us (69%)
  blocking collectives  65.6 us (25%)
  local copies, waits for them, and re-layouts  11.2 us (4%)
    pallas_call x1, Pallas kernels, on_device(): pl.pallas_call(kernel, out_shape=(jax.ShapeDtypeStruct((rows, QH * HD), b...  180 us
    psum x1, blocking collectives, on_device(): sums = lax.psum(jnp.concatenate([qgp, kgp], axis=0), ('dp', 'seq'))  65.6 us
    unnamed x16, local copies, waits for them, and re-layouts  11.2 us

profile of v1, /device:TPU:0, one launch (start us, length us, event | category | flops | bytes accessed | tf_op | source)
XLA Modules:
  0.0 258.1 jit_solution(4008306878914613927)
XLA Ops:
  0.6 0.0 copy-start
  0.7 0.8 copy-done
  1.5 0.0 copy-start.2
  1.5 0.9 copy-done.2
  2.4 0.0 copy-start.3
  2.4 0.9 copy-done.3
  3.4 0.0 copy-start.4
  3.4 0.7 copy-done.4
  4.0 0.0 copy-start.5
  4.0 0.7 copy-done.5
  4.7 180.1 %exchange_attend.1 = (bf16[128,8192]{1,0:T(8,128)(2,1)S(1)}, bf16[128,8192]{1,0:T(8,128)(2,1)S(1)}, bf16[128,1024]{1,0:T(8,128)(2,1)S(1)}, bf16[128,1024]{1,0:T(...) custom-call(bf16[128,8192]{1,0:T(8,128)(2,1)} %q.1, bf16[128,1024]{1,0:T(8,128)(2,1)S(1)} %copy-done.2, ...), custom_call_target="tpu_custom_call" | custom-call | flops 20000000000 | bytes 20000000 | tf_op jit(solution)/shard_map/exchange_attend/pallas_call | solution.py:375
  184.8 0.0 copy-start.1
  184.9 1.3 copy-done.1
  186.2 65.6 %psum.7 = f32[2,128]{1,0:T(2,128)S(1)} all-reduce(f32[2,128]{1,0:T(2,128)S(1)} %pad_maximum_fusion), channel_id=1, replica_groups=mesh['dp'=8,'seq'=16] {'dp','seq'}, use_global_device_ids=true, to_apply=%region_0.1 | all-reduce | flops 256 | bytes 2048 | tf_op jit(solution)/shard_map/psum | solution.py:424
  251.8 0.5 multiply_bitcast_fusion
  252.3 3.1 %copy.17 = bf16[128,8192]{1,0:T(8,128)(2,1)} copy(bf16[128,8192]{1,0:T(8,128)(2,1)} %copy-done.1) | data formatting | bytes 4194304
  255.4 1.3 copy.18
  256.7 0.7 copy.19
  257.4 0.7 copy.20
  (2 shorter events, 0.0 us)
Async XLA Ops:
  0.6 0.8 copy-start
  1.5 0.9 copy-start.2
  2.4 0.9 copy-start.3
  3.4 0.7 copy-start.4
  4.0 0.7 copy-start.5
  184.8 1.3 copy-start.1

commit v2 on v1

--- a/solution.py
+++ b/solution.py
@@ -14,11 +14,12 @@
 NEG = -1e30
 MESH = pl.DeviceIdType.MESH
 BLK = 128
+ROWS = 8
 SIDE = 4
 PART = 4096
 OWN = 1024
-CH = 512
-KT = 256
+HEADS = 8
+KT = 512
 SCALE = 1.0 / math.sqrt(HD)
 LOG2E = math.log2(math.e)
 bf16 = jnp.bfloat16
@@ -41,8 +42,8 @@
 def kernel(
     q, k, v, do, seg, qg, kg,
     o, dq, dk, dv, qgp, kgp,
-    qs, ds_, kv, kn, vn, kt_, vt_, os_, dqs, es, ms, firsts, dka, dva, sb, rb, fb, qn, ot, dqt, gacc,
-    s_in, r_in, s_kv, r_kv, s_ag, r_ag, s_out, r_out, s_rs, r_rs, s_f, r_f,
+    qs, ds_, kv, kn, vn, kt_, vt_, os_, dqs, es, ms, firsts, dka, dva, sb, rb, fb, qn, ot, dqt, gacc, gb,
+    s_in, r_in, s_kv, r_kv, s_ag, r_ag, s_out, r_out, s_rs, r_rs, s_f, r_f, s_g, r_g,
 ):
     seq = lax.axis_index("seq")
     dp = lax.axis_index("dp")
@@ -63,12 +64,19 @@
     def cols(start, width):
         return pl.ds(pl.multiple_of(start, width), width)
 
+    def dev_of(p, j):
+        return (dp, j * SIDE + y) if p == 0 else (dp, x * SIDE + j)
+
     barrier = pltpu.get_barrier_semaphore()
     for p in (0, 1):
         for d in (1, 2, 3):
-            j = (mine[p] + d) % SIDE
-            dev = (dp, j * SIDE + y) if p == 0 else (dp, x * SIDE + j)
-            pl.semaphore_signal(barrier, inc=1, device_id=dev, device_id_type=MESH)
+            pl.semaphore_signal(
+                barrier, inc=1, device_id=dev_of(p, (mine[p] + d) % SIDE), device_id_type=MESH
+            )
+    for d in range(1, ROWS):
+        pl.semaphore_signal(
+            barrier, inc=1, device_id=((dp + d) % ROWS, seq), device_id_type=MESH
+        )
 
     for p in (0, 1):
         me = mine[p]
@@ -76,10 +84,7 @@
             pltpu.make_async_copy(
                 src.at[:, cols(p * 512 + me * HD, HD)], kv.at[p, i, x, y], r_kv.at[p, i, me]
             ).start()
-    pl.semaphore_wait(barrier, 6)
-
-    def dev_of(p, j):
-        return (dp, j * SIDE + y) if p == 0 else (dp, x * SIDE + j)
+    pl.semaphore_wait(barrier, 6 + ROWS - 1)
 
     kv_sends = []
     for d in (1, 3, 2):
@@ -98,11 +103,9 @@
         me = mine[p]
         for i, src in enumerate((q, do)):
             dst = (qs, ds_)[i]
-            for c in (0, 1):
-                pltpu.make_async_copy(
-                    src.at[:, cols(p * PART + me * OWN + c * CH, CH)],
-                    dst.at[p, me, c], r_in.at[i, p, me, c],
-                ).start()
+            pltpu.make_async_copy(
+                src.at[:, cols(p * PART + me * OWN, OWN)], dst.at[p, me], r_in.at[i, p, me]
+            ).start()
 
     ag_sends = []
     for p in (0, 1):
@@ -121,21 +124,20 @@
             ag_sends.append(c)
 
     in_sends = []
-    for c in (0, 1):
-        for d in (1, 3, 2):
-            for p in (0, 1):
-                me = mine[p]
-                j = (me + d) % SIDE
-                for i, src in enumerate((q, do)):
-                    dst = (qs, ds_)[i]
-                    cp = remote(
-                        src.at[:, cols(p * PART + j * OWN + c * CH, CH)], dst.at[p, me, c],
-                        s_in.at[i, p, d, c], r_in.at[i, p, me, c], dev_of(p, j),
-                    )
-                    cp.start()
-                    in_sends.append(cp)
-
-    ids = seg[...]
+    for d in (1, 3, 2):
+        for p in (0, 1):
+            me = mine[p]
+            j = (me + d) % SIDE
+            for i, src in enumerate((q, do)):
+                dst = (qs, ds_)[i]
+                c = remote(
+                    src.at[:, cols(p * PART + j * OWN, OWN)], dst.at[p, me],
+                    s_in.at[i, p, d], r_in.at[i, p, me], dev_of(p, j),
+                )
+                c.start()
+                in_sends.append(c)
+
+    ids = seg[dp]
     first = jnp.zeros((16, BLK), jnp.int32)
     for value in range(7):
         hits = jnp.where(ids == value, 1, 0)
@@ -172,23 +174,22 @@
     lax.fori_loop(0, 32, prep, 0)
 
     def unit(u, carry):
-        c = u // 8
         p = u % 2
-        step = (u % 8) // 2
+        step = u // 2
         d = lax.select(step == 2, 3, lax.select(step == 3, 2, step))
         me = own(p)
         j = (me + d) % SIDE
         b = lax.select(p == 0, j * SIDE + y, x * SIDE + j)
-        n_tiles = b // 2 + 1
+        n_tiles = b // (KT // BLK) + 1
         for i, dst in enumerate((qs, ds_)):
-            blk = dst.at[p, j, c]
-            pltpu.make_async_copy(blk, blk, r_in.at[i, p, j, c]).wait()
-
-        for h in range(4):
-            raw = qs[p, j, c, :, h * HD : (h + 1) * HD].astype(f32)
+            blk = dst.at[p, j]
+            pltpu.make_async_copy(blk, blk, r_in.at[i, p, j]).wait()
+
+        for h in range(HEADS):
+            raw = qs[p, j, :, h * HD : (h + 1) * HD].astype(f32)
             inv = lax.rsqrt(jnp.mean(raw * raw, axis=-1, keepdims=True) + EPS)
             qn[0, h * BLK : (h + 1) * BLK, :] = (raw * inv * qg[...]).astype(bf16)
-            qn[1, h * BLK : (h + 1) * BLK, :] = ds_[p, j, c, :, h * HD : (h + 1) * HD]
+            qn[1, h * BLK : (h + 1) * BLK, :] = ds_[p, j, :, h * HD : (h + 1) * HD]
 
         q_pos = b * BLK + lax.broadcasted_iota(jnp.int32, (1, BLK), 1)
         q_first = firsts[b]
@@ -200,7 +201,7 @@
             k_pos = t * KT + lax.broadcasted_iota(jnp.int32, (KT, BLK), 0)
             allowed = (k_pos >= q_first) & (k_pos <= q_pos)
             s = jnp.concatenate(
-                [jnp.where(allowed, s[:, h * BLK : (h + 1) * BLK], NEG) for h in range(4)], axis=1
+                [jnp.where(allowed, s[:, h * BLK : (h + 1) * BLK], NEG) for h in range(HEADS)], axis=1
             )
             new = jnp.maximum(top, jnp.max(fold(s, jnp.max), axis=0, keepdims=True))
             e = jnp.exp2((s - new) * (SCALE * LOG2E))
@@ -210,7 +211,7 @@
             return new, total
 
         top, total = lax.fori_loop(
-            0, n_tiles, scores, (jnp.full((1, CH), NEG, f32), jnp.zeros((8, CH), f32))
+            0, n_tiles, scores, (jnp.full((1, OWN), NEG, f32), jnp.zeros((8, OWN), f32))
         )
         recip = 1.0 / jnp.sum(total, axis=0, keepdims=True)
 
@@ -219,9 +220,7 @@
         def outs(t, carry):
             rows = cols(t * KT, KT)
             factor = jnp.exp2((ms[t] - top) * (SCALE * LOG2E)) * recip
-            e = es[rows, :] * factor
-            es[rows, :] = e
-            pr = e.astype(bf16)
+            pr = (es[rows, :] * factor).astype(bf16)
             ot[...] += dot_nn(vt_[p, :, rows], pr)
             dva[p, rows, :] += dot_nn(pr, qn[1])
             return carry
@@ -229,9 +228,9 @@
         lax.fori_loop(0, n_tiles, outs, 0)
 
         deltas = []
-        for h in range(4):
+        for h in range(HEADS):
             out = ot[:, h * BLK : (h + 1) * BLK].T.astype(bf16)
-            os_[p, j, c, :, h * HD : (h + 1) * HD] = out
+            os_[p, j, :, h * HD : (h + 1) * HD] = out
             up = qn[1, h * BLK : (h + 1) * BLK, :].astype(f32)
             deltas.append(jnp.sum((up * out.astype(f32)).T, axis=0, keepdims=True))
         delta = jnp.concatenate(deltas, axis=1)
@@ -241,41 +240,42 @@
         def grads(t, carry):
             rows = cols(t * KT, KT)
             dp_ = dot_nt(vn[p, rows, :], qn[1])
-            g = (es[rows, :] * (dp_ - delta) * SCALE).astype(bf16)
+            factor = jnp.exp2((ms[t] - top) * (SCALE * LOG2E)) * (recip * SCALE)
+            g = ((es[rows, :] * factor) * (dp_ - delta)).astype(bf16)
             dqt[...] += dot_nn(kt_[p, :, rows], g)
             dka[p, rows, :] += dot_nn(g, qn[0])
             return carry
 
         lax.fori_loop(0, n_tiles, grads, 0)
 
-        for h in range(4):
-            raw = qs[p, j, c, :, h * HD : (h + 1) * HD].astype(f32)
+        for h in range(HEADS):
+            raw = qs[p, j, :, h * HD : (h + 1) * HD].astype(f32)
             inv = lax.rsqrt(jnp.mean(raw * raw, axis=-1, keepdims=True) + EPS)
             hat = raw * inv
             grad = dqt[:, h * BLK : (h + 1) * BLK].T
             gacc[0] += fold(grad * hat, jnp.sum)
             g = grad * qg[...]
-            dqs[p, j, c, :, h * HD : (h + 1) * HD] = (
+            dqs[p, j, :, h * HD : (h + 1) * HD] = (
                 inv * (g - hat * jnp.mean(g * hat, axis=-1, keepdims=True))
             ).astype(bf16)
 
         for i, (src, dst) in enumerate(((os_, o), (dqs, dq))):
-            place = dst.at[:, cols(p * PART + me * OWN + c * CH, CH)]
+            place = dst.at[:, cols(p * PART + me * OWN, OWN)]
 
             @pl.when(d == 0)
             def _():
-                pltpu.make_async_copy(src.at[p, j, c], place, r_out.at[i, p, j, c]).start()
+                pltpu.make_async_copy(src.at[p, j], place, r_out.at[i, p, j]).start()
 
             @pl.when(d != 0)
             def _():
                 remote(
-                    src.at[p, j, c], place, s_out.at[i, p, d, c], r_out.at[i, p, me, c],
+                    src.at[p, j], place, s_out.at[i, p, d], r_out.at[i, p, me],
                     where(p, j),
                 ).start()
 
         return carry
 
-    lax.fori_loop(0, 16, unit, 0)
+    lax.fori_loop(0, 8, unit, 0)
 
     def pack(t, carry):
         p, b = t // 16, t % 16
@@ -334,27 +334,47 @@
                     c.start()
                     f_sends.append(c)
 
-    qgp[...] = jnp.sum(gacc[0], axis=0, keepdims=True)
-    kgp[...] = jnp.sum(gacc[1], axis=0, keepdims=True)
-
-    for c in kv_sends + ag_sends + in_sends + rs_sends + f_sends:
+    held = jnp.concatenate(
+        [jnp.sum(gacc[i], axis=0, keepdims=True) for i in (0, 1)] + [jnp.zeros((6, HD), f32)],
+        axis=0,
+    )
+    g_sends = []
+    for n, (place, count) in enumerate(((x, SIDE), (y, SIDE), (dp, ROWS))):
+        gb[n, place] = held
+        for d in range(1, count):
+            j = (place + d) % count
+            dev = dev_of(n, j) if n < 2 else (j, seq)
+            c = remote(gb.at[n, place], gb.at[n, place], s_g.at[n, d], r_g.at[n, place], dev)
+            c.start()
+            g_sends.append(c)
+        for d in range(1, count):
+            blk = gb.at[n, (place + d) % count]
+            pltpu.make_async_copy(blk, blk, r_g.at[n, (place + d) % count]).wait()
+        held = gb[n, 0]
+        for j in range(1, count):
+            held = held + gb[n, j]
+    tokens = ROWS * SIDE * SIDE * BLK
+    qgp[...] = held[0:1] / math.sqrt(tokens * QH)
+    kgp[...] = held[1:2] / math.sqrt(tokens * KVH)
+
+    for c in kv_sends + ag_sends + in_sends + rs_sends + f_sends + g_sends:
         c.wait_send()
 
     def drain(t, carry):
-        i, p, d, c = t // 12, (t // 6) % 2, (t // 2) % 3 + 1, t % 2
-        src = os_.at[0, 0, 0]
-        pltpu.make_async_copy(src, src, s_out.at[i, p, d, c]).wait()
+        i, p, d = t // 6, (t // 3) % 2, t % 3 + 1
+        src = os_.at[0, 0]
+        pltpu.make_async_copy(src, src, s_out.at[i, p, d]).wait()
         return carry
 
-    lax.fori_loop(0, 24, drain, 0)
+    lax.fori_loop(0, 12, drain, 0)
 
     def arrive(t, carry):
-        i, p, j, c = t // 16, (t // 8) % 2, (t // 2) % 4, t % 2
-        place = o.at[:, cols(p * PART + j * OWN + c * CH, CH)]
-        pltpu.make_async_copy(place, place, r_out.at[i, p, j, c]).wait()
+        i, p, j = t // 8, (t // 4) % 2, t % 4
+        place = o.at[:, cols(p * PART + j * OWN, OWN)]
+        pltpu.make_async_copy(place, place, r_out.at[i, p, j]).wait()
         return carry
 
-    lax.fori_loop(0, 32, arrive, 0)
+    lax.fori_loop(0, 16, arrive, 0)
     for p in (0, 1):
         for i, dst in enumerate((dk, dv)):
             for j in range(SIDE):
@@ -364,10 +384,7 @@
 
 def on_device(q_proj, k_proj, v_proj, q_gain, k_gain, dout, segments):
     rows = q_proj.shape[0]
-    total_rows = rows * lax.axis_size("seq") * lax.axis_size("dp")
-    ids = lax.dynamic_index_in_dim(
-        segments.reshape(lax.axis_size("dp"), 16, BLK), lax.axis_index("dp"), 0, keepdims=False
-    )
+    ids = segments.reshape(ROWS, SIDE * SIDE, BLK)
     any_ = pl.BlockSpec(memory_space=pl.ANY)
     vmem = pl.BlockSpec(memory_space=pltpu.VMEM)
     dma = pltpu.SemaphoreType.DMA
@@ -385,51 +402,45 @@
         in_specs=[any_, any_, any_, any_, vmem, vmem, vmem],
         out_specs=(any_, any_, any_, any_, vmem, vmem),
         scratch_shapes=[
-            pltpu.VMEM((2, SIDE, 2, BLK, CH), bf16),
-            pltpu.VMEM((2, SIDE, 2, BLK, CH), bf16),
+            pltpu.VMEM((2, SIDE, BLK, OWN), bf16),
+            pltpu.VMEM((2, SIDE, BLK, OWN), bf16),
             pltpu.VMEM((2, 2, SIDE, SIDE, BLK, HD), bf16),
             pltpu.VMEM((2, length, HD), bf16),
             pltpu.VMEM((2, length, HD), bf16),
             pltpu.VMEM((2, HD, length), bf16),
             pltpu.VMEM((2, HD, length), bf16),
-            pltpu.VMEM((2, SIDE, 2, BLK, CH), bf16),
-            pltpu.VMEM((2, SIDE, 2, BLK, CH), bf16),
-            pltpu.VMEM((length, CH), f32),
-            pltpu.VMEM((8, 1, CH), f32),
+            pltpu.VMEM((2, SIDE, BLK, OWN), bf16),
+            pltpu.VMEM((2, SIDE, BLK, OWN), bf16),
+            pltpu.VMEM((length, OWN), f32),
+            pltpu.VMEM((SIDE, 1, OWN), f32),
             pltpu.VMEM((16, 1, BLK), jnp.int32),
             pltpu.VMEM((2, length, HD), f32),
             pltpu.VMEM((2, length, HD), f32),
             pltpu.VMEM((2, 2, SIDE, SIDE, BLK, HD), bf16),
             pltpu.VMEM((2, SIDE, 2, SIDE, BLK, HD), bf16),
             pltpu.VMEM((2, 2, SIDE, BLK, HD), bf16),
-            pltpu.VMEM((2, CH, HD), bf16),
-            pltpu.VMEM((HD, CH), f32),
-            pltpu.VMEM((HD, CH), f32),
+            pltpu.VMEM((2, OWN, HD), bf16),
+            pltpu.VMEM((HD, OWN), f32),
+            pltpu.VMEM((HD, OWN), f32),
             pltpu.VMEM((2, 8, HD), f32),
-            dma((2, 2, SIDE, 2)), dma((2, 2, SIDE, 2)),
+            pltpu.VMEM((3, ROWS, 8, HD), f32),
+            dma((2, 2, SIDE)), dma((2, 2, SIDE)),
             dma((2, 2, SIDE)), dma((2, 2, SIDE)),
             dma((2, SIDE)), dma((2, SIDE)),
-            dma((2, 2, SIDE, 2)), dma((2, 2, SIDE, 2)),
+            dma((2, 2, SIDE)), dma((2, 2, SIDE)),
             dma((2, SIDE)), dma((2, SIDE)),
             dma((2, 2, SIDE)), dma((2, 2, SIDE)),
+            dma((3, ROWS)), dma((3, ROWS)),
         ],
         name="exchange_attend",
         cost_estimate=pl.CostEstimate(
             flops=20_000_000_000, bytes_accessed=20_000_000, transcendentals=10_000_000
         ),
         compiler_params=pltpu.CompilerParams(
-            collective_id=0, has_side_effects=True, vmem_limit_bytes=48 << 20
+            collective_id=0, has_side_effects=True, vmem_limit_bytes=58 << 20
         ),
     )(q_proj, k_proj, v_proj, dout, ids, q_gain.reshape(1, HD), k_gain.reshape(1, HD))
-    sums = lax.psum(jnp.concatenate([qgp, kgp], axis=0), ("dp", "seq"))
-    return (
-        o,
-        dq,
-        dk,
-        dv,
-        sums[0] / math.sqrt(total_rows * QH),
-        sums[1] / math.sqrt(total_rows * KVH),
-    )
+    return o, dq, dk, dv, qgp.reshape(HD), kgp.reshape(HD)
 
 
 def solution(mesh):

time: 259 us -> 158 us (0.61)
  blocking collectives: 65.6 us -> 0 us
  Pallas kernels: 180 us -> 149 us
  local copies, waits for them, and re-layouts: 11.2 us -> 7.01 us
    psum x1 -> x0, blocking collectives: 65.6 us -> none  [on_device(): sums = lax.psum(jnp.concatenate([qgp, kgp], axis=0), ('dp', 'seq'))]
    pallas_call x1, Pallas kernels: 180 us -> 149 us  [on_device(): pl.pallas_call(kernel, out_shape=(jax.ShapeDtypeStruct((rows, QH * HD), b...]
    unnamed x16, local copies, waits for them, and re-layouts: 11.2 us -> 7.01 us
where the time goes in v2:
time: 158 us; the launch traced here: 157 us
  Pallas kernels  149 us (94%)
  local copies, waits for them, and re-layouts  7.01 us (4%)
    pallas_call x1, Pallas kernels, on_device(): pl.pallas_call(kernel, out_shape=(jax.ShapeDtypeStruct((rows, QH * HD), b...  149 us
    unnamed x16, local copies, waits for them, and re-layouts  7.01 us

profile of v2, /device:TPU:0, one launch (start us, length us, event | category | flops | bytes accessed | tf_op | source)
XLA Modules:
  0.0 156.9 jit_solution(4019816608978322990)
XLA Ops:
  0.6 149.2 %exchange_attend.1 = (bf16[128,8192]{1,0:T(8,128)(2,1)}, bf16[128,8192]{1,0:T(8,128)(2,1)}, bf16[128,1024]{1,0:T(8,128)(2,1)}, bf16[128,1024]{1,0:T(8,128)(2,1)}, f32[1,128]{1,0:T(1,128)}, /*index=5*/f32[1,128]{1,0:T(1,128)}) custom-call(bf16[128,8192]{1,0:T(8,128)(2,1)} %q.1, bf16[128,1024]{1,0:T(8,128)(2,1)} %k.1, bf16[128,1024]{1,0:T(8,128)(2,1)} %v.1, ...), custom_call_target="tpu_custom_call" | custom-call | flops 20000000000 | bytes 20000000 | tf_op jit(solution)/shard_map/exchange_attend/pallas_call | solution.py:392
  149.9 0.0 copy-start
  149.9 3.2 %copy.19 = bf16[128,8192]{1,0:T(8,128)(2,1)} copy(bf16[128,8192]{1,0:T(8,128)(2,1)} %get-tuple-element.24) | data formatting | bytes 4194304
  153.1 0.0 copy-done
  153.1 0.0 copy-start.2
  153.1 0.0 copy-start.1
  153.1 0.0 copy-start.4
  153.1 0.0 copy-start.3
  153.1 1.3 copy.20
  154.5 0.0 copy-done.2
  154.5 0.7 copy.21
  155.2 0.0 copy-done.1
  155.2 0.7 copy.22
  155.9 0.0 copy-done.4
  155.9 0.5 copy.23
  156.4 0.0 copy-done.3
  156.4 0.5 copy.24
Async XLA Ops:
  149.9 3.3 %copy-start = (bf16[128,8192]{1,0:T(8,128)(2,1)S(1)}, bf16[128,8192]{1,0:T(8,128)(2,1)}, u32[]{:S(2)}) copy-start(bf16[128,8192]{1,0:T(8,128)(2,1)} %get-tuple-element.25) | copy-start | bytes 6291460
  153.1 1.3 copy-start.2
  153.1 2.0 %copy-start.1 = (bf16[128,1024]{1,0:T(8,128)(2,1)S(1)}, bf16[128,1024]{1,0:T(8,128)(2,1)}, u32[]{:S(2)}) copy-start(bf16[128,1024]{1,0:T(8,128)(2,1)} %get-tuple-element.27) | copy-start | bytes 786436
  153.1 2.8 %copy-start.4 = (f32[1,128]{1,0:T(1,128)S(1)}, f32[1,128]{1,0:T(1,128)}, u32[]{:S(2)}) copy-start(f32[1,128]{1,0:T(1,128)} %get-tuple-element.16) | copy-start | bytes 1540
  153.1 3.3 %copy-start.3 = (f32[1,128]{1,0:T(1,128)S(1)}, f32[1,128]{1,0:T(1,128)}, u32[]{:S(2)}) copy-start(f32[1,128]{1,0:T(1,128)} %get-tuple-element.17) | copy-start | bytes 1540

commit v3 on v2

--- a/solution.py
+++ b/solution.py
@@ -1,3 +1,4 @@
+import functools
 import math
 
 import jax
@@ -20,6 +21,7 @@
 OWN = 1024
 HEADS = 8
 KT = 512
+EARLY = (1,)
 SCALE = 1.0 / math.sqrt(HD)
 LOG2E = math.log2(math.e)
 bf16 = jnp.bfloat16
@@ -50,9 +52,6 @@
     x, y = seq // SIDE, seq % SIDE
     mine = (x, y)
 
-    def where(p, j):
-        return (dp, lax.select(p == 0, j * SIDE + y, x * SIDE + j))
-
     def own(p):
         return lax.select(p == 0, x, y)
 
@@ -87,11 +86,11 @@
     pl.semaphore_wait(barrier, 6 + ROWS - 1)
 
     kv_sends = []
-    for d in (1, 3, 2):
-        for p in (0, 1):
-            me = mine[p]
-            j = (me + d) % SIDE
-            for i, src in enumerate((k, v)):
+    for i, src in enumerate((k, v)):
+        for d in (1, 3, 2):
+            for p in (0, 1):
+                me = mine[p]
+                j = (me + d) % SIDE
                 c = remote(
                     src.at[:, cols(p * 512 + j * HD, HD)], kv.at[p, i, x, y],
                     s_kv.at[p, i, d], r_kv.at[p, i, me], dev_of(p, j),
@@ -108,23 +107,24 @@
             ).start()
 
     ag_sends = []
-    for p in (0, 1):
-        me = mine[p]
-        other = mine[1 - p]
-        for j in range(SIDE):
-            for i in (0, 1):
+    for i in (0, 1):
+        for p in (0, 1):
+            other = mine[1 - p]
+            for j in range(SIDE):
                 blk = kv.at[p, i, j, y] if p == 0 else kv.at[p, i, x, j]
                 pltpu.make_async_copy(blk, blk, r_kv.at[p, i, j]).wait()
-        held = kv.at[0, :, :, y] if p == 0 else kv.at[1, :, x]
-        for d in (1, 3, 2):
-            c = remote(
-                held, held, s_ag.at[p, d], r_ag.at[p, other], dev_of(1 - p, (other + d) % SIDE)
-            )
-            c.start()
-            ag_sends.append(c)
+            held = kv.at[0, i, :, y] if p == 0 else kv.at[1, i, x]
+            for d in (1, 3, 2):
+                c = remote(
+                    held, held, s_ag.at[p, i, d], r_ag.at[p, i, other],
+                    dev_of(1 - p, (other + d) % SIDE),
+                )
+                c.start()
+                ag_sends.append(c)
 
     in_sends = []
-    for d in (1, 3, 2):
+
+    def send_in(d):
         for p in (0, 1):
             me = mine[p]
             j = (me + d) % SIDE
@@ -137,6 +137,9 @@
                 c.start()
                 in_sends.append(c)
 
+    for d in EARLY:
+        send_in(d)
+
     ids = seg[dp]
     first = jnp.zeros((16, BLK), jnp.int32)
     for value in range(7):
@@ -151,27 +154,56 @@
     for i in range(16):
         firsts[i] = seg_first[i : i + 1, :]
 
-    for p in (0, 1):
+    def prep(p, i, place):
+        def block(n, carry):
+            xb, yb = (n, place) if p == 0 else (place, n)
+            rows = cols((xb * SIDE + yb) * BLK, BLK)
+            if i == 0:
+                raw = kv[p, 0, xb, yb].astype(f32)
+                inv = lax.rsqrt(jnp.mean(raw * raw, axis=-1, keepdims=True) + EPS)
+                normed = (raw * inv * kg[...]).astype(bf16)
+                kn[p, rows, :] = normed
+                kt_[p, :, rows] = normed.astype(f32).T.astype(bf16)
+            else:
+                val = kv[p, 1, xb, yb]
+                vn[p, rows, :] = val
+                vt_[p, :, rows] = val.astype(f32).T.astype(bf16)
+            return carry
+
+        lax.fori_loop(0, SIDE, block, 0)
+
+    def gathered(i):
+        for p in (0, 1):
+            prep(p, i, mine[1 - p])
+        for d in (1, 3, 2):
+            for p in (0, 1):
+                j = (mine[1 - p] + d) % SIDE
+                blk = kv.at[0, i, :, j] if p == 0 else kv.at[1, i, j]
+                pltpu.make_async_copy(blk, blk, r_ag.at[p, i, j]).wait()
+                prep(p, i, j)
+
+    gathered(0)
+    for d in (1, 3, 2):
+        if d not in EARLY:
+            send_in(d)
+
+    def share(p, i):
+        acc = (dka, dva)[i]
+
+        def pack(b, carry):
+            sb[p, i, b // SIDE, b % SIDE] = acc[p, cols(b * BLK, BLK), :].astype(bf16)
+            return carry
+
+        lax.fori_loop(0, SIDE * SIDE, pack, 0)
         other = mine[1 - p]
         for d in (1, 3, 2):
             j = (other + d) % SIDE
-            blk = kv.at[0, :, :, j] if p == 0 else kv.at[1, :, j]
-            pltpu.make_async_copy(blk, blk, r_ag.at[p, j]).wait()
-
-    def prep(t, carry):
-        p, b = t // 16, t % 16
-        raw = kv[p, 0, b // SIDE, b % SIDE].astype(f32)
-        inv = lax.rsqrt(jnp.mean(raw * raw, axis=-1, keepdims=True) + EPS)
-        normed = (raw * inv * kg[...]).astype(bf16)
-        rows = cols(b * BLK, BLK)
-        kn[p, rows, :] = normed
-        kt_[p, :, rows] = normed.astype(f32).T.astype(bf16)
-        val = kv[p, 1, b // SIDE, b % SIDE]
-        vn[p, rows, :] = val
-        vt_[p, :, rows] = val.astype(f32).T.astype(bf16)
-        return carry
-
-    lax.fori_loop(0, 32, prep, 0)
+            src = sb.at[0, i, :, j] if p == 0 else sb.at[1, i, j]
+            remote(
+                src, rb.at[p, other, i], s_rs.at[p, i, d], r_rs.at[p, i, other], dev_of(1 - p, j)
+            ).start()
+
+    last_of = (6, 7)
 
     def unit(u, carry):
         p = u % 2
@@ -214,6 +246,7 @@
             0, n_tiles, scores, (jnp.full((1, OWN), NEG, f32), jnp.zeros((8, OWN), f32))
         )
         recip = 1.0 / jnp.sum(total, axis=0, keepdims=True)
+        pl.when(u == 0)(functools.partial(gathered, 1))
 
         ot[...] = jnp.zeros_like(ot)
 
@@ -226,6 +259,21 @@
             return carry
 
         lax.fori_loop(0, n_tiles, outs, 0)
+        for part in (0, 1):
+            pl.when(u == last_of[part])(functools.partial(share, part, 1))
+
+        def send_out(i, src, dst):
+            place = dst.at[:, cols(p * PART + me * OWN, OWN)]
+
+            @pl.when(d == 0)
+            def _():
+                pltpu.make_async_copy(src.at[p, j], place, r_out.at[i, p, j]).start()
+
+            @pl.when(d != 0)
+            def _():
+                remote(
+                    src.at[p, j], place, s_out.at[i, p, d], r_out.at[i, p, me], (dp, b)
+                ).start()
 
         deltas = []
         for h in range(HEADS):
@@ -234,6 +282,7 @@
             up = qn[1, h * BLK : (h + 1) * BLK, :].astype(f32)
             deltas.append(jnp.sum((up * out.astype(f32)).T, axis=0, keepdims=True))
         delta = jnp.concatenate(deltas, axis=1)
+        send_out(0, os_, o)
 
         dqt[...] = jnp.zeros_like(dqt)
 
@@ -247,6 +296,8 @@
             return carry
 
         lax.fori_loop(0, n_tiles, grads, 0)
+        for part in (0, 1):
+            pl.when(u == last_of[part])(functools.partial(share, part, 0))
 
         for h in range(HEADS):
             raw = qs[p, j, :, h * HD : (h + 1) * HD].astype(f32)
@@ -259,51 +310,63 @@
                 inv * (g - hat * jnp.mean(g * hat, axis=-1, keepdims=True))
             ).astype(bf16)
 
-        for i, (src, dst) in enumerate(((os_, o), (dqs, dq))):
-            place = dst.at[:, cols(p * PART + me * OWN, OWN)]
-
-            @pl.when(d == 0)
-            def _():
-                pltpu.make_async_copy(src.at[p, j], place, r_out.at[i, p, j]).start()
-
-            @pl.when(d != 0)
-            def _():
-                remote(
-                    src.at[p, j], place, s_out.at[i, p, d], r_out.at[i, p, me],
-                    where(p, j),
-                ).start()
+        send_out(1, dqs, dq)
 
         return carry
 
     lax.fori_loop(0, 8, unit, 0)
 
-    def pack(t, carry):
+    def key_gain(t, carry):
         p, b = t // 16, t % 16
-        rows = cols(b * BLK, BLK)
-        sb[p, 0, b // SIDE, b % SIDE] = dka[p, rows, :].astype(bf16)
-        sb[p, 1, b // SIDE, b % SIDE] = dva[p, rows, :].astype(bf16)
+        raw = kv[p, 0, b // SIDE, b % SIDE].astype(f32)
+        inv = lax.rsqrt(jnp.mean(raw * raw, axis=-1, keepdims=True) + EPS)
+        gacc[1] += fold(dka[p, cols(b * BLK, BLK), :] * (raw * inv), jnp.sum)
         return carry
 
-    rs_sends = []
-    for p in (0, 1):
-        lax.fori_loop(p * 16, p * 16 + 16, pack, 0)
-        other = mine[1 - p]
-        for d in (1, 3, 2):
-            j = (other + d) % SIDE
-            src = sb.at[0, :, :, j] if p == 0 else sb.at[1, :, j]
-            c = remote(
-                src, rb.at[p, other], s_rs.at[p, d], r_rs.at[p, other], dev_of(1 - p, j)
-            )
+    lax.fori_loop(0, 32, key_gain, 0)
+
+    g_sends = []
+    stages = ((dp, ROWS), (x, SIDE), (y, SIDE))
+
+    def gain_send(n, held):
+        place, count = stages[n]
+        gb[n, place] = held
+        for d in range(1, count):
+            j = (place + d) % count
+            dev = (j, seq) if n == 0 else dev_of(n - 1, j)
+            c = remote(gb.at[n, place], gb.at[n, place], s_g.at[n, d], r_g.at[n, place], dev)
             c.start()
-            rs_sends.append(c)
+            g_sends.append(c)
+
+    def gain_sum(n):
+        place, count = stages[n]
+        for d in range(1, count):
+            blk = gb.at[n, (place + d) % count]
+            pltpu.make_async_copy(blk, blk, r_g.at[n, (place + d) % count]).wait()
+        held = gb[n, 0]
+        for j in range(1, count):
+            held = held + gb[n, j]
+        return held
+
+    gain_send(
+        0,
+        jnp.concatenate(
+            [jnp.sum(gacc[i], axis=0, keepdims=True) for i in (0, 1)]
+            + [jnp.zeros((6, HD), f32)],
+            axis=0,
+        ),
+    )
+    gain_send(1, gain_sum(0))
 
     f_sends = []
     for p in (0, 1):
         other = mine[1 - p]
         me = mine[p]
         for d in (1, 3, 2):
-            blk = rb.at[p, (other + d) % SIDE]
-            pltpu.make_async_copy(blk, blk, r_rs.at[p, (other + d) % SIDE]).wait()
+            slot = (other + d) % SIDE
+            for i in (0, 1):
+                blk = rb.at[p, slot, i]
+                pltpu.make_async_copy(blk, blk, r_rs.at[p, i, slot]).wait()
         for dd in (1, 3, 2, 0):
             j = (me + dd) % SIDE
             b = j * SIDE + y if p == 0 else x * SIDE + j
@@ -317,7 +380,6 @@
             raw = (kv[0, 0, j, y] if p == 0 else kv[1, 0, x, j]).astype(f32)
             inv = lax.rsqrt(jnp.mean(raw * raw, axis=-1, keepdims=True) + EPS)
             hat = raw * inv
-            gacc[1] += fold(kgrad * hat, jnp.sum)
             g = kgrad * kg[...]
             fb[p, 0, j] = (inv * (g - hat * jnp.mean(g * hat, axis=-1, keepdims=True))).astype(
                 bf16
@@ -334,30 +396,13 @@
                     c.start()
                     f_sends.append(c)
 
-    held = jnp.concatenate(
-        [jnp.sum(gacc[i], axis=0, keepdims=True) for i in (0, 1)] + [jnp.zeros((6, HD), f32)],
-        axis=0,
-    )
-    g_sends = []
-    for n, (place, count) in enumerate(((x, SIDE), (y, SIDE), (dp, ROWS))):
-        gb[n, place] = held
-        for d in range(1, count):
-            j = (place + d) % count
-            dev = dev_of(n, j) if n < 2 else (j, seq)
-            c = remote(gb.at[n, place], gb.at[n, place], s_g.at[n, d], r_g.at[n, place], dev)
-            c.start()
-            g_sends.append(c)
-        for d in range(1, count):
-            blk = gb.at[n, (place + d) % count]
-            pltpu.make_async_copy(blk, blk, r_g.at[n, (place + d) % count]).wait()
-        held = gb[n, 0]
-        for j in range(1, count):
-            held = held + gb[n, j]
+    gain_send(2, gain_sum(1))
+    held = gain_sum(2)
     tokens = ROWS * SIDE * SIDE * BLK
     qgp[...] = held[0:1] / math.sqrt(tokens * QH)
     kgp[...] = held[1:2] / math.sqrt(tokens * KVH)
 
-    for c in kv_sends + ag_sends + in_sends + rs_sends + f_sends + g_sends:
+    for c in kv_sends + ag_sends + in_sends + f_sends + g_sends:
         c.wait_send()
 
     def drain(t, carry):
@@ -367,6 +412,12 @@
         return carry
 
     lax.fori_loop(0, 12, drain, 0)
+
+    for p in (0, 1):
+        for i in (0, 1):
+            for d in (1, 2, 3):
+                blk = rb.at[0, 0, 0]
+                pltpu.make_async_copy(blk, blk, s_rs.at[p, i, d]).wait()
 
     def arrive(t, carry):
         i, p, j = t // 8, (t // 4) % 2, t % 4
@@ -426,9 +477,9 @@
             pltpu.VMEM((3, ROWS, 8, HD), f32),
             dma((2, 2, SIDE)), dma((2, 2, SIDE)),
             dma((2, 2, SIDE)), dma((2, 2, SIDE)),
-            dma((2, SIDE)), dma((2, SIDE)),
             dma((2, 2, SIDE)), dma((2, 2, SIDE)),
-            dma((2, SIDE)), dma((2, SIDE)),
+            dma((2, 2, SIDE)), dma((2, 2, SIDE)),
+            dma((2, 2, SIDE)), dma((2, 2, SIDE)),
             dma((2, 2, SIDE)), dma((2, 2, SIDE)),
             dma((3, ROWS)), dma((3, ROWS)),
         ],

time: 158 us -> 131 us (0.83)
  Pallas kernels: 149 us -> 123 us
    pallas_call x1, Pallas kernels: 149 us -> 123 us  [on_device(): pl.pallas_call(kernel, out_shape=(jax.ShapeDtypeStruct((rows, QH * HD), b...]
where the time goes in v3:
time: 131 us
  Pallas kernels  123 us (94%)
  local copies, waits for them, and re-layouts  7.01 us (5%)
    pallas_call x1, Pallas kernels, on_device(): pl.pallas_call(kernel, out_shape=(jax.ShapeDtypeStruct((rows, QH * HD), b...  123 us
    unnamed x16, local copies, waits for them, and re-layouts  7.01 us

profile of v3, /device:TPU:0, one launch (start us, length us, event | category | flops | bytes accessed | tf_op | source)
XLA Modules:
  0.0 130.8 jit_solution(977001312873179316)
XLA Ops:
  0.6 123.1 %exchange_attend.1 = (bf16[128,8192]{1,0:T(8,128)(2,1)}, bf16[128,8192]{1,0:T(8,128)(2,1)}, bf16[128,1024]{1,0:T(8,128)(2,1)}, bf16[128,1024]{1,0:T(8,128)(2,1)}, f32[1,128]{1,0:T(1,128)}, /*index=5*/f32[1,128]{1,0:T(1,128)}) custom-call(bf16[128,8192]{1,0:T(8,128)(2,1)} %q.1, bf16[128,1024]{1,0:T(8,128)(2,1)} %k.1, bf16[128,1024]{1,0:T(8,128)(2,1)} %v.1, ...), custom_call_target="tpu_custom_call" | custom-call | flops 20000000000 | bytes 20000000 | tf_op jit(solution)/shard_map/exchange_attend/pallas_call | solution.py:443
  123.8 0.0 copy-start
  123.8 3.2 %copy.19 = bf16[128,8192]{1,0:T(8,128)(2,1)} copy(bf16[128,8192]{1,0:T(8,128)(2,1)} %get-tuple-element.24) | data formatting | bytes 4194304
  127.0 0.0 copy-done
  127.0 0.0 copy-start.2
  127.0 0.0 copy-start.1
  127.0 0.0 copy-start.4
  127.0 0.0 copy-start.3
  127.0 1.3 %copy.20 = bf16[128,8192]{1,0:T(8,128)(2,1)} copy(bf16[128,8192]{1,0:T(8,128)(2,1)S(1)} %copy-done) | data formatting | bytes 4194304
  128.4 0.0 copy-done.2
  128.4 0.7 copy.21
  129.1 0.0 copy-done.1
  129.1 0.7 copy.22
  129.8 0.0 copy-done.4
  129.8 0.5 copy.23
  130.3 0.0 copy-done.3
  130.3 0.5 copy.24
Async XLA Ops:
  123.8 3.3 %copy-start = (bf16[128,8192]{1,0:T(8,128)(2,1)S(1)}, bf16[128,8192]{1,0:T(8,128)(2,1)}, u32[]{:S(2)}) copy-start(bf16[128,8192]{1,0:T(8,128)(2,1)} %get-tuple-element.25) | copy-start | bytes 6291460
  127.0 1.3 %copy-start.2 = (bf16[128,1024]{1,0:T(8,128)(2,1)S(1)}, bf16[128,1024]{1,0:T(8,128)(2,1)}, u32[]{:S(2)}) copy-start(bf16[128,1024]{1,0:T(8,128)(2,1)} %get-tuple-element.26) | copy-start | bytes 786436
  127.0 2.0 %copy-start.1 = (bf16[128,1024]{1,0:T(8,128)(2,1)S(1)}, bf16[128,1024]{1,0:T(8,128)(2,1)}, u32[]{:S(2)}) copy-start(bf16[128,1024]{1,0:T(8,128)(2,1)} %get-tuple-element.27) | copy-start | bytes 786436
  127.0 2.8 %copy-start.4 = (f32[1,128]{1,0:T(1,128)S(1)}, f32[1,128]{1,0:T(1,128)}, u32[]{:S(2)}) copy-start(f32[1,128]{1,0:T(1,128)} %get-tuple-element.16) | copy-start | bytes 1540
  127.0 3.3 %copy-start.3 = (f32[1,128]{1,0:T(1,128)S(1)}, f32[1,128]{1,0:T(1,128)}, u32[]{:S(2)}) copy-start(f32[1,128]{1,0:T(1,128)} %get-tuple-element.17) | copy-start | bytes 1540

commit v4 on v3

--- a/solution.py
+++ b/solution.py
@@ -41,6 +41,24 @@
     return op(x.reshape(rows // 8, 8, cols), axis=0)
 
 
+def in_pairs(step, count):
+    def pair(n, carry):
+        step(2 * n, 2)
+        return carry
+
+    def single(n, carry):
+        step(count - 1, 1)
+        return carry
+
+    def quad(n, carry):
+        step(0, 4)
+        return carry
+
+    lax.fori_loop(0, count // 4, quad, 0)
+    lax.fori_loop(0, count % 4 // 2, pair, 0)
+    lax.fori_loop(0, count % 2, single, 0)
+
+
 def kernel(
     q, k, v, do, seg, qg, kg,
     o, dq, dk, dv, qgp, kgp,
@@ -61,7 +79,7 @@
         )
 
     def cols(start, width):
-        return pl.ds(pl.multiple_of(start, width), width)
+        return pl.ds(pl.multiple_of(start, min(width, KT)), width)
 
     def dev_of(p, j):
         return (dp, j * SIDE + y) if p == 0 else (dp, x * SIDE + j)
@@ -226,39 +244,57 @@
         q_pos = b * BLK + lax.broadcasted_iota(jnp.int32, (1, BLK), 1)
         q_first = firsts[b]
 
-        def scores(t, carry):
+        def scores(first, tiles, carry):
             top, total = carry
-            rows = cols(t * KT, KT)
-            s = dot_nt(kn[p, rows, :], qn[0])
-            k_pos = t * KT + lax.broadcasted_iota(jnp.int32, (KT, BLK), 0)
-            allowed = (k_pos >= q_first) & (k_pos <= q_pos)
-            s = jnp.concatenate(
-                [jnp.where(allowed, s[:, h * BLK : (h + 1) * BLK], NEG) for h in range(HEADS)], axis=1
-            )
-            new = jnp.maximum(top, jnp.max(fold(s, jnp.max), axis=0, keepdims=True))
-            e = jnp.exp2((s - new) * (SCALE * LOG2E))
-            es[rows, :] = e
-            ms[t] = new
-            total = total * jnp.exp2((top - new) * (SCALE * LOG2E)) + fold(e, jnp.sum)
+            found = []
+            for n in range(tiles):
+                t = first + n
+                s = dot_nt(kn[p, cols(t * KT, KT), :], qn[0])
+                k_pos = t * KT + lax.broadcasted_iota(jnp.int32, (KT, BLK), 0)
+                allowed = (k_pos >= q_first) & (k_pos <= q_pos)
+                found.append(
+                    jnp.concatenate(
+                        [
+                            jnp.where(allowed, s[:, h * BLK : (h + 1) * BLK], NEG)
+                            for h in range(HEADS)
+                        ],
+                        axis=1,
+                    )
+                )
+            new = top
+            for s in found:
+                new = jnp.maximum(new, jnp.max(fold(s, jnp.max), axis=0, keepdims=True))
+            total = total * jnp.exp2((top - new) * (SCALE * LOG2E))
+            for n in range(tiles):
+                t, s = first + n, found[n]
+                e = jnp.exp2((s - new) * (SCALE * LOG2E))
+                es[cols(t * KT, KT), :] = e
+                ms[t] = new
+                total = total + fold(e, jnp.sum)
             return new, total
 
+        carry_ = (jnp.full((1, OWN), NEG, f32), jnp.zeros((8, OWN), f32))
+        carry_ = lax.fori_loop(0, n_tiles // 2, lambda n, c: scores(2 * n, 2, c), carry_)
         top, total = lax.fori_loop(
-            0, n_tiles, scores, (jnp.full((1, OWN), NEG, f32), jnp.zeros((8, OWN), f32))
+            0, n_tiles % 2, lambda n, c: scores(n_tiles - 1, 1, c), carry_
         )
         recip = 1.0 / jnp.sum(total, axis=0, keepdims=True)
         pl.when(u == 0)(functools.partial(gathered, 1))
 
         ot[...] = jnp.zeros_like(ot)
 
-        def outs(t, carry):
-            rows = cols(t * KT, KT)
-            factor = jnp.exp2((ms[t] - top) * (SCALE * LOG2E)) * recip
-            pr = (es[rows, :] * factor).astype(bf16)
+        def outs(first, tiles):
+            rows = cols(first * KT, tiles * KT)
+            parts = []
+            for n in range(tiles):
+                t = first + n
+                factor = jnp.exp2((ms[t] - top) * (SCALE * LOG2E)) * recip
+                parts.append((es[cols(t * KT, KT), :] * factor).astype(bf16))
+            pr = jnp.concatenate(parts, axis=0)
             ot[...] += dot_nn(vt_[p, :, rows], pr)
             dva[p, rows, :] += dot_nn(pr, qn[1])
-            return carry
-
-        lax.fori_loop(0, n_tiles, outs, 0)
+
+        in_pairs(outs, n_tiles)
         for part in (0, 1):
             pl.when(u == last_of[part])(functools.partial(share, part, 1))
 
@@ -275,6 +311,7 @@
                     src.at[p, j], place, s_out.at[i, p, d], r_out.at[i, p, me], (dp, b)
                 ).start()
 
+        ones = jnp.ones((8, HD), bf16)
         deltas = []
         for h in range(HEADS):
             out = ot[:, h * BLK : (h + 1) * BLK].T.astype(bf16)
@@ -286,16 +323,20 @@
 
         dqt[...] = jnp.zeros_like(dqt)
 
-        def grads(t, carry):
-            rows = cols(t * KT, KT)
-            dp_ = dot_nt(vn[p, rows, :], qn[1])
-            factor = jnp.exp2((ms[t] - top) * (SCALE * LOG2E)) * (recip * SCALE)
-            g = ((es[rows, :] * factor) * (dp_ - delta)).astype(bf16)
+        def grads(first, tiles):
+            rows = cols(first * KT, tiles * KT)
+            parts = []
+            for n in range(tiles):
+                t = first + n
+                own_rows = cols(t * KT, KT)
+                dprob = dot_nt(vn[p, own_rows, :], qn[1])
+                factor = jnp.exp2((ms[t] - top) * (SCALE * LOG2E)) * (recip * SCALE)
+                parts.append(((es[own_rows, :] * factor) * (dprob - delta)).astype(bf16))
+            g = jnp.concatenate(parts, axis=0)
             dqt[...] += dot_nn(kt_[p, :, rows], g)
             dka[p, rows, :] += dot_nn(g, qn[0])
-            return carry
-
-        lax.fori_loop(0, n_tiles, grads, 0)
+
+        in_pairs(grads, n_tiles)
         for part in (0, 1):
             pl.when(u == last_of[part])(functools.partial(share, part, 0))
 

time: 131 us -> 123 us (0.939)
  Pallas kernels: 123 us -> 115 us
    pallas_call x1, Pallas kernels: 123 us -> 115 us  [on_device(): pl.pallas_call(kernel, out_shape=(jax.ShapeDtypeStruct((rows, QH * HD), b...]
where the time goes in v4:
time: 123 us
  Pallas kernels  115 us (93%)
  local copies, waits for them, and re-layouts  7.01 us (6%)
    pallas_call x1, Pallas kernels, on_device(): pl.pallas_call(kernel, out_shape=(jax.ShapeDtypeStruct((rows, QH * HD), b...  115 us
    unnamed x16, local copies, waits for them, and re-layouts  7.01 us

profile of v4, /device:TPU:0, one launch (start us, length us, event | category | flops | bytes accessed | tf_op | source)
XLA Modules:
  0.0 123.0 jit_solution(6396117527492168091)
XLA Ops:
  0.6 115.3 %exchange_attend.1 = (bf16[128,8192]{1,0:T(8,128)(2,1)}, bf16[128,8192]{1,0:T(8,128)(2,1)}, bf16[128,1024]{1,0:T(8,128)(2,1)}, bf16[128,1024]{1,0:T(8,128)(2,1)}, f32[1,128]{1,0:T(1,128)}, /*index=5*/f32[1,128]{1,0:T(1,128)}) custom-call(bf16[128,8192]{1,0:T(8,128)(2,1)} %q.1, bf16[128,1024]{1,0:T(8,128)(2,1)} %k.1, bf16[128,1024]{1,0:T(8,128)(2,1)} %v.1, ...), custom_call_target="tpu_custom_call" | custom-call | flops 20000000000 | bytes 20000000 | tf_op jit(solution)/shard_map/exchange_attend/pallas_call | solution.py:484
  115.9 0.0 copy-start
  115.9 3.2 %copy.19 = bf16[128,8192]{1,0:T(8,128)(2,1)} copy(bf16[128,8192]{1,0:T(8,128)(2,1)} %get-tuple-element.24) | data formatting | bytes 4194304
  119.2 0.0 copy-done
  119.2 0.0 copy-start.2
  119.2 0.0 copy-start.1
  119.2 0.0 copy-start.4
  119.2 0.0 copy-start.3
  119.2 1.3 %copy.20 = bf16[128,8192]{1,0:T(8,128)(2,1)} copy(bf16[128,8192]{1,0:T(8,128)(2,1)S(1)} %copy-done) | data formatting | bytes 4194304
  120.5 0.0 copy-done.2
  120.5 0.7 copy.21
  121.2 0.0 copy-done.1
  121.2 0.7 copy.22
  121.9 0.0 copy-done.4
  121.9 0.5 copy.23
  122.4 0.0 copy-done.3
  122.4 0.5 copy.24
Async XLA Ops:
  115.9 3.3 %copy-start = (bf16[128,8192]{1,0:T(8,128)(2,1)S(1)}, bf16[128,8192]{1,0:T(8,128)(2,1)}, u32[]{:S(2)}) copy-start(bf16[128,8192]{1,0:T(8,128)(2,1)} %get-tuple-element.25) | copy-start | bytes 6291460
  119.2 1.3 %copy-start.2 = (bf16[128,1024]{1,0:T(8,128)(2,1)S(1)}, bf16[128,1024]{1,0:T(8,128)(2,1)}, u32[]{:S(2)}) copy-start(bf16[128,1024]{1,0:T(8,128)(2,1)} %get-tuple-element.26) | copy-start | bytes 786436
  119.2 2.0 %copy-start.1 = (bf16[128,1024]{1,0:T(8,128)(2,1)S(1)}, bf16[128,1024]{1,0:T(8,128)(2,1)}, u32[]{:S(2)}) copy-start(bf16[128,1024]{1,0:T(8,128)(2,1)} %get-tuple-element.27) | copy-start | bytes 786436
  119.2 2.8 %copy-start.4 = (f32[1,128]{1,0:T(1,128)S(1)}, f32[1,128]{1,0:T(1,128)}, u32[]{:S(2)}) copy-start(f32[1,128]{1,0:T(1,128)} %get-tuple-element.16) | copy-start | bytes 1540
  119.2 3.3 %copy-start.3 = (f32[1,128]{1,0:T(1,128)S(1)}, f32[1,128]{1,0:T(1,128)}, u32[]{:S(2)}) copy-start(f32[1,128]{1,0:T(1,128)} %get-tuple-element.17) | copy-start | bytes 1540

commit v5 on v4

--- a/solution.py
+++ b/solution.py
@@ -274,7 +274,8 @@
             return new, total
 
         carry_ = (jnp.full((1, OWN), NEG, f32), jnp.zeros((8, OWN), f32))
-        carry_ = lax.fori_loop(0, n_tiles // 2, lambda n, c: scores(2 * n, 2, c), carry_)
+        carry_ = lax.fori_loop(0, n_tiles // 4, lambda n, c: scores(0, 4, c), carry_)
+        carry_ = lax.fori_loop(0, n_tiles % 4 // 2, lambda n, c: scores(0, 2, c), carry_)
         top, total = lax.fori_loop(
             0, n_tiles % 2, lambda n, c: scores(n_tiles - 1, 1, c), carry_
         )

time: 123 us -> 122 us (level)
    pallas_call x1, Pallas kernels: 115 us -> 114 us  [on_device(): pl.pallas_call(kernel, out_shape=(jax.ShapeDtypeStruct((rows, QH * HD), b...]
where the time goes in v5:
time: 122 us
  Pallas kernels  114 us (93%)
  local copies, waits for them, and re-layouts  7.01 us (6%)
    pallas_call x1, Pallas kernels, on_device(): pl.pallas_call(kernel, out_shape=(jax.ShapeDtypeStruct((rows, QH * HD), b...  114 us
    unnamed x16, local copies, waits for them, and re-layouts  7.01 us

profile of v5, /device:TPU:0, one launch (start us, length us, event | category | flops | bytes accessed | tf_op | source)
XLA Modules:
  0.0 121.6 jit_solution(13635131809651841642)
XLA Ops:
  0.6 113.9 %exchange_attend.1 = (bf16[128,8192]{1,0:T(8,128)(2,1)}, bf16[128,8192]{1,0:T(8,128)(2,1)}, bf16[128,1024]{1,0:T(8,128)(2,1)}, bf16[128,1024]{1,0:T(8,128)(2,1)}, f32[1,128]{1,0:T(1,128)}, /*index=5*/f32[1,128]{1,0:T(1,128)}) custom-call(bf16[128,8192]{1,0:T(8,128)(2,1)} %q.1, bf16[128,1024]{1,0:T(8,128)(2,1)} %k.1, bf16[128,1024]{1,0:T(8,128)(2,1)} %v.1, ...), custom_call_target="tpu_custom_call" | custom-call | flops 20000000000 | bytes 20000000 | tf_op jit(solution)/shard_map/exchange_attend/pallas_call | solution.py:485
  114.6 0.0 copy-start
  114.6 3.2 %copy.19 = bf16[128,8192]{1,0:T(8,128)(2,1)} copy(bf16[128,8192]{1,0:T(8,128)(2,1)} %get-tuple-element.24) | data formatting | bytes 4194304
  117.8 0.0 copy-done
  117.8 0.0 copy-start.2
  117.8 0.0 copy-start.1
  117.8 0.0 copy-start.4
  117.8 0.0 copy-start.3
  117.8 1.3 %copy.20 = bf16[128,8192]{1,0:T(8,128)(2,1)} copy(bf16[128,8192]{1,0:T(8,128)(2,1)S(1)} %copy-done) | data formatting | bytes 4194304
  119.2 0.0 copy-done.2
  119.2 0.7 copy.21
  119.9 0.0 copy-done.1
  119.9 0.7 copy.22
  120.6 0.0 copy-done.4
  120.6 0.5 copy.23
  121.1 0.0 copy-done.3
  121.1 0.5 copy.24
Async XLA Ops:
  114.6 3.3 %copy-start = (bf16[128,8192]{1,0:T(8,128)(2,1)S(1)}, bf16[128,8192]{1,0:T(8,128)(2,1)}, u32[]{:S(2)}) copy-start(bf16[128,8192]{1,0:T(8,128)(2,1)} %get-tuple-element.25) | copy-start | bytes 6291460
  117.8 1.3 %copy-start.2 = (bf16[128,1024]{1,0:T(8,128)(2,1)S(1)}, bf16[128,1024]{1,0:T(8,128)(2,1)}, u32[]{:S(2)}) copy-start(bf16[128,1024]{1,0:T(8,128)(2,1)} %get-tuple-element.26) | copy-start | bytes 786436
  117.8 2.0 %copy-start.1 = (bf16[128,1024]{1,0:T(8,128)(2,1)S(1)}, bf16[128,1024]{1,0:T(8,128)(2,1)}, u32[]{:S(2)}) copy-start(bf16[128,1024]{1,0:T(8,128)(2,1)} %get-tuple-element.27) | copy-start | bytes 786436
  117.8 2.8 %copy-start.4 = (f32[1,128]{1,0:T(1,128)S(1)}, f32[1,128]{1,0:T(1,128)}, u32[]{:S(2)}) copy-start(f32[1,128]{1,0:T(1,128)} %get-tuple-element.16) | copy-start | bytes 1540
  117.8 3.3 %copy-start.3 = (f32[1,128]{1,0:T(1,128)S(1)}, f32[1,128]{1,0:T(1,128)}, u32[]{:S(2)}) copy-start(f32[1,128]{1,0:T(1,128)} %get-tuple-element.17) | copy-start | bytes 1540

commit v6 on v5

--- a/solution.py
+++ b/solution.py
@@ -140,8 +140,6 @@
                 c.start()
                 ag_sends.append(c)
 
-    in_sends = []
-
     def send_in(d):
         for p in (0, 1):
             me = mine[p]
@@ -153,7 +151,6 @@
                     s_in.at[i, p, d], r_in.at[i, p, me], dev_of(p, j),
                 )
                 c.start()
-                in_sends.append(c)
 
     for d in EARLY:
         send_in(d)
@@ -201,9 +198,6 @@
                 prep(p, i, j)
 
     gathered(0)
-    for d in (1, 3, 2):
-        if d not in EARLY:
-            send_in(d)
 
     def share(p, i):
         acc = (dka, dva)[i]
@@ -280,7 +274,13 @@
             0, n_tiles % 2, lambda n, c: scores(n_tiles - 1, 1, c), carry_
         )
         recip = 1.0 / jnp.sum(total, axis=0, keepdims=True)
-        pl.when(u == 0)(functools.partial(gathered, 1))
+
+        @pl.when(u == 0)
+        def _():
+            gathered(1)
+            for d in (3, 2):
+                send_in(d)
+
 
         ot[...] = jnp.zeros_like(ot)
 
@@ -444,13 +444,14 @@
     qgp[...] = held[0:1] / math.sqrt(tokens * QH)
     kgp[...] = held[1:2] / math.sqrt(tokens * KVH)
 
-    for c in kv_sends + ag_sends + in_sends + f_sends + g_sends:
+    for c in kv_sends + ag_sends + f_sends + g_sends:
         c.wait_send()
 
     def drain(t, carry):
         i, p, d = t // 6, (t // 3) % 2, t % 3 + 1
         src = os_.at[0, 0]
         pltpu.make_async_copy(src, src, s_out.at[i, p, d]).wait()
+        pltpu.make_async_copy(src, src, s_in.at[i, p, d]).wait()
         return carry
 
     lax.fori_loop(0, 12, drain, 0)

time: 122 us -> 122 us (level)
  no operation moved by 1% of the time
where the time goes in v6:
time: 122 us
  Pallas kernels  114 us (93%)
  local copies, waits for them, and re-layouts  7.01 us (6%)
    pallas_call x1, Pallas kernels, on_device(): pl.pallas_call(kernel, out_shape=(jax.ShapeDtypeStruct((rows, QH * HD), b...  114 us
    unnamed x16, local copies, waits for them, and re-layouts  7.01 us

profile of v6, /device:TPU:0, one launch (start us, length us, event | category | flops | bytes accessed | tf_op | source)
XLA Modules:
  0.0 121.7 jit_solution(11034133959820431683)
XLA Ops:
  0.6 114.0 %exchange_attend.1 = (bf16[128,8192]{1,0:T(8,128)(2,1)}, bf16[128,8192]{1,0:T(8,128)(2,1)}, bf16[128,1024]{1,0:T(8,128)(2,1)}, bf16[128,1024]{1,0:T(8,128)(2,1)}, f32[1,128]{1,0:T(1,128)}, /*index=5*/f32[1,128]{1,0:T(1,128)}) custom-call(bf16[128,8192]{1,0:T(8,128)(2,1)} %q.1, bf16[128,1024]{1,0:T(8,128)(2,1)} %k.1, bf16[128,1024]{1,0:T(8,128)(2,1)} %v.1, ...), custom_call_target="tpu_custom_call" | custom-call | flops 20000000000 | bytes 20000000 | tf_op jit(solution)/shard_map/exchange_attend/pallas_call | solution.py:486
  114.6 0.0 copy-start
  114.6 3.2 %copy.19 = bf16[128,8192]{1,0:T(8,128)(2,1)} copy(bf16[128,8192]{1,0:T(8,128)(2,1)} %get-tuple-element.24) | data formatting | bytes 4194304
  117.9 0.0 copy-done
  117.9 0.0 copy-start.2
  117.9 0.0 copy-start.1
  117.9 0.0 copy-start.4
  117.9 0.0 copy-start.3
  117.9 1.3 %copy.20 = bf16[128,8192]{1,0:T(8,128)(2,1)} copy(bf16[128,8192]{1,0:T(8,128)(2,1)S(1)} %copy-done) | data formatting | bytes 4194304
  119.2 0.0 copy-done.2
  119.2 0.7 copy.21
  119.9 0.0 copy-done.1
  119.9 0.7 copy.22
  120.6 0.0 copy-done.4
  120.6 0.5 copy.23
  121.1 0.0 copy-done.3
  121.1 0.5 copy.24
Async XLA Ops:
  114.6 3.3 %copy-start = (bf16[128,8192]{1,0:T(8,128)(2,1)S(1)}, bf16[128,8192]{1,0:T(8,128)(2,1)}, u32[]{:S(2)}) copy-start(bf16[128,8192]{1,0:T(8,128)(2,1)} %get-tuple-element.25) | copy-start | bytes 6291460
  117.9 1.3 %copy-start.2 = (bf16[128,1024]{1,0:T(8,128)(2,1)S(1)}, bf16[128,1024]{1,0:T(8,128)(2,1)}, u32[]{:S(2)}) copy-start(bf16[128,1024]{1,0:T(8,128)(2,1)} %get-tuple-element.26) | copy-start | bytes 786436
  117.9 2.0 %copy-start.1 = (bf16[128,1024]{1,0:T(8,128)(2,1)S(1)}, bf16[128,1024]{1,0:T(8,128)(2,1)}, u32[]{:S(2)}) copy-start(bf16[128,1024]{1,0:T(8,128)(2,1)} %get-tuple-element.27) | copy-start | bytes 786436
  117.9 2.8 %copy-start.4 = (f32[1,128]{1,0:T(1,128)S(1)}, f32[1,128]{1,0:T(1,128)}, u32[]{:S(2)}) copy-start(f32[1,128]{1,0:T(1,128)} %get-tuple-element.16) | copy-start | bytes 1540
  117.9 3.3 %copy-start.3 = (f32[1,128]{1,0:T(1,128)S(1)}, f32[1,128]{1,0:T(1,128)}, u32[]{:S(2)}) copy-start(f32[1,128]{1,0:T(1,128)} %get-tuple-element.17) | copy-start | bytes 1540
